TPU v7x, 256 devices: a whole 4x4x8 slice. The times are simulated.
256 devices in a mesh: lat: 32 (over z_hi, x, core), lev: 8 (over z_lo, y).
Axes of the slice: x: 4, y: 4, z: 8 (z_hi: 4, z_lo: 2; z = z_hi * 2 + z_lo), core: 2. Of those that a mesh axis runs over, the one named last changes fastest.
Arguments:
- velocity: float32 [2, 32, 256, 1152], P(None, 'lev', 'lat'), may hold values from -0.6 to 0.6
- potential_temp: float32 [32, 256, 1152], P('lev', 'lat'), may hold values from 0.5 to 1.5
- tracer: float32 [32, 256, 1152], P('lev', 'lat'), may hold values from 0.1 to 1
- thickness: float32 [32, 256, 1152], P('lev', 'lat'), may hold values from 0.5 to 1.5
- surface_height: float32 [256, 1152], P('lat'), may hold values from 0 to 1
- level_fractions: float32 [32], replicated, may hold values from 0.25 to 4
Outputs:
- remapped: float32 [4, 32, 256, 1152], P(None, 'lev', 'lat')
- new_thickness: float32 [32, 256, 1152], P('lev', 'lat')
- geopotential: float32 [32, 256, 1152], P('lev', 'lat')
All inputs are finite; a program needn't handle non-finite values.
Results may differ from a plain program's by a relative error of at most 0.0003.
Values sent between devices are 32-bit elements; how exact they have to be, the bound alone decides.
A program may use at most 64 MiB of HBM per device.

v0:
```python
import jax
import jax.numpy as jnp
from jax import lax
from jax.sharding import PartitionSpec as P

SUBSTEPS = 4


ADVECT = 0.3
PRESS = 0.15
ROTATION_RATE = 0.3
TOP_PRESSURE = 1.0


def with_halo(array, sides, width):
    for axis, dim in sides:
        devices, length = (lax.axis_size(axis), array.shape[dim])
        up = [(i, (i + 1) % devices) for i in range(devices - 1)]
        down = [(j, i) for i, j in up]
        last = lax.slice_in_dim(array, length - width, length, axis=dim)
        leading = lax.slice_in_dim(array, 0, width, axis=dim)
        before = lax.ppermute(last, axis, up)
        after = lax.ppermute(leading, axis, down)
        array = jnp.concatenate([before, array, after], axis=dim)
    return array


def zonal_slope(values):
    return (
        8.0 * (jnp.roll(values, -1, -1) - jnp.roll(values, 1, -1))
        - (jnp.roll(values, -2, -1) - jnp.roll(values, 2, -1))
    ) / 12.0


def polar_slope(padded):
    return (
        8.0 * (padded[..., 3:-1, :] - padded[..., 1:-3, :])
        - (padded[..., 4:, :] - padded[..., :-4, :])
    ) / 12.0


def coriolis(row_ids, latitude_strip_summation):
    angle = -0.5 * jnp.pi + (row_ids.astype(jnp.float32) + 0.5) * (
        jnp.pi / latitude_strip_summation
    )
    return (ROTATION_RATE * jnp.sin(angle))[:, None]


def substep(padded, turning):
    interior = padded[..., 2:-2, :]
    east_slope = zonal_slope(interior)
    north_slope = polar_slope(padded)
    eastward = interior[0]
    northward = interior[1]
    carried = ADVECT * (eastward * east_slope + northward * north_slope)
    new_east = eastward - carried[0] - PRESS * east_slope[4] + turning * northward
    new_north = northward - carried[1] - PRESS * north_slope[4] - turning * eastward
    new_temp = interior[2] - carried[2]
    new_tracer = interior[3] - carried[3]
    new_log = interior[4] - carried[4] - ADVECT * (east_slope[0] + north_slope[1])
    return jnp.stack([new_east, new_north, new_temp, new_tracer, new_log], 0)


def remap_flat(flat_fields, level_fractions):
    values = flat_fields[:4]
    layer_thick = flat_fields[4]
    levels = layer_thick.shape[0]
    lower_edge = jnp.cumsum(layer_thick, axis=0)
    upper_edge = lower_edge - layer_thick
    bottom_pressure = lower_edge[-1]
    portion = level_fractions / jnp.sum(level_fractions)
    bounds = jnp.concatenate([jnp.zeros((1,), jnp.float32), jnp.cumsum(portion)])
    target_interfaces = bottom_pressure[None] * bounds[:, None]

    def add_layer(level, integral):
        top_here = lax.dynamic_slice_in_dim(upper_edge, level, 1, 0)
        thick_here = lax.dynamic_slice_in_dim(layer_thick, level, 1, 0)
        value_here = lax.dynamic_slice_in_dim(values, level, 1, 1)
        covered = jnp.clip(target_interfaces - top_here, 0.0, thick_here)
        return integral + value_here * covered[None]

    integral = lax.fori_loop(
        0, levels, add_layer, jnp.zeros((4,) + target_interfaces.shape, jnp.float32)
    )
    new_thickness = bottom_pressure[None] * portion[:, None]
    remapped = (integral[:, 1:] - integral[:, :-1]) / new_thickness[None]
    return (remapped, new_thickness, target_interfaces)


def vertical_stack_heights(thermal_state_field, target_interfaces, terrain_floor):
    atmospheric_stress_field = TOP_PRESSURE + target_interfaces
    sheet_thickness_delta = thermal_state_field * jnp.log(
        atmospheric_stress_field[1:] / atmospheric_stress_field[:-1]
    )
    return terrain_floor[None] + jnp.flip(jnp.cumsum(jnp.flip(sheet_thickness_delta, 0), 0), 0)


def shards(velocity, potential_temp, tracer, thickness, surface_height, level_fractions):
    gridded_quantities = jnp.concatenate(
        [velocity, potential_temp[None], tracer[None], jnp.log(thickness)[None]], 0
    )
    row_count = gridded_quantities.shape[2]
    latitude_strip_summation = row_count * lax.axis_size("lat")
    first_row = lax.axis_index("lat") * row_count
    turning = coriolis(first_row + jnp.arange(row_count, dtype=jnp.int32), latitude_strip_summation)
    for repeat in range(SUBSTEPS):
        padded = with_halo(gridded_quantities, (("lat", 2),), 2)
        gridded_quantities = substep(padded, turning)
    advanced = jnp.concatenate([gridded_quantities[:4], jnp.exp(gridded_quantities[4:])], 0)
    columns = lax.all_to_all(advanced, "lev", split_axis=3, concat_axis=1, tiled=True)
    field_count, levels, row_span, block_span = columns.shape
    flat_fields = columns.reshape((field_count, levels, row_span * block_span))
    remapped_flat, thick_flat, target_interfaces = remap_flat(flat_fields, level_fractions)
    remapped = remapped_flat.reshape((4, levels, row_span, block_span))
    new_thickness = thick_flat.reshape((levels, row_span, block_span))
    terrain_floor = lax.dynamic_slice_in_dim(
        surface_height, lax.axis_index("lev") * block_span, block_span, 1
    )
    heights_flat = vertical_stack_heights(
        remapped_flat[2], target_interfaces, terrain_floor.reshape((row_span * block_span,))
    )
    heights = heights_flat.reshape((levels, row_span, block_span))
    returned = lax.all_to_all(
        jnp.concatenate([remapped, new_thickness[None], heights[None]], 0),
        "lev",
        split_axis=1,
        concat_axis=3,
        tiled=True,
    )
    return (returned[:4], returned[4], returned[5])


def solution(mesh):
    return jax.shard_map(
        shards,
        mesh=mesh,
        in_specs=(
            P(None, "lev", "lat", None),
            P("lev", "lat", None),
            P("lev", "lat", None),
            P("lev", "lat", None),
            P("lat", None),
            P(),
        ),
        out_specs=(P(None, "lev", "lat", None), P("lev", "lat", None), P("lev", "lat", None)),
        check_vma=False,
    )
```

profile of v0, /device:TPU:128, one launch (start us, length us, event | category | flops | bytes accessed | tf_op | source)
XLA Modules:
  0.0 188.8 jit_solution(4604562805182064390)
XLA Ops:
  0.6 0.9 log_bitcast_fusion
  1.6 0.7 copy-done.5
  2.3 1.2 pad_maximum_fusion.8
  3.5 0.7 copy.122
  4.3 3.2 %collective-permute-start = (f32[5,4,2,1152]{3,1,2,0:T(4,128)}, f32[5,4,2,1152]{3,1,2,0:T(4,128)}, u32[]{:S(2)}, u32[]{:S(2)}) collective-permute-start(f32[5,4,2,1152]{3,1,2,0:T(4,128)} %copy.122), channel_id=1, source_target_pairs={{8,0},{16,8},{24,16},{32,24},{40,32},{48,40},{56,48},{64,56},{72,6... | collective-permute-start | bytes 552968 | tf_op jit(solution)/shard_map/ppermute | solution.py:23
  7.5 0.7 copy.123
  8.2 1.9 %collective-permute-start.1 = (f32[5,4,2,1152]{3,1,2,0:T(4,128)}, f32[5,4,2,1152]{3,1,2,0:T(4,128)}, u32[]{:S(2)}, u32[]{:S(2)}) collective-permute-start(f32[5,4,2,1152]{3,1,2,0:T(4,128)} %copy.123), channel_id=1, source_target_pairs={{0,8},{8,16},{16,24},{24,32},{32,40},{40,48},{48,56},{56,64},{64,7... | collective-permute-start | bytes 552968 | tf_op jit(solution)/shard_map/ppermute | solution.py:22
  10.4 1.1 fusion.120
  11.5 0.7 fusion.119
  12.2 0.7 multiply_bitcast_fusion.7
  13.1 1.0 copy.95
  14.1 7.4 %collective-permute-done.1 = f32[5,4,2,1152]{3,1,2,0:T(4,128)} collective-permute-done((f32[5,4,2,1152]{3,1,2,0:T(4,128)}, f32[5,4,2,1152]{3,1,2,0:T(4,128)}, u32[]{:S(2)}, u32[]{:S(2)}) %collective-permute-start.1) | collective-permute-done | bytes 184352 | tf_op jit(solution)/shard_map/ppermute | solution.py:22
  21.5 1.0 copy.97
  22.5 1.4 pad_maximum_fusion.1
  24.3 0.8 copy-done.2
  25.2 0.6 add_multiply_fusion.3
  26.0 0.7 copy-done.4
  27.7 1.9 %collective-permute-start.3 = (f32[5,4,2,1152]{3,1,2,0:T(4,128)S(1)}, f32[5,4,2,1152]{3,1,2,0:T(4,128)S(1)}, u32[]{:S(2)}, u32[]{:S(2)}) collective-permute-start(f32[5,4,2,1152]{3,1,2,0:T(4,128)S(1)} %copy.125), channel_id=1, source_target_pairs={{0,8},{8,16},{16,24},{24,32},{32,40},{40,48},{48,56},{56,64},{64,7... | collective-permute-start | bytes 552968 | tf_op jit(solution)/shard_map/ppermute | solution.py:22
  29.6 7.9 %collective-permute-start.2 = (f32[5,4,2,1152]{3,1,2,0:T(4,128)S(1)}, f32[5,4,2,1152]{3,1,2,0:T(4,128)S(1)}, u32[]{:S(2)}, u32[]{:S(2)}) collective-permute-start(f32[5,4,2,1152]{3,1,2,0:T(4,128)S(1)} %copy.124), channel_id=1, source_target_pairs={{8,0},{16,8},{24,16},{32,24},{40,32},{48,40},{56,48},{64,56},{72,6... | collective-permute-start | bytes 552968 | tf_op jit(solution)/shard_map/ppermute | solution.py:23
  37.6 1.2 collective-permute-done.3
  38.9 2.1 %collective-permute-done.2 = f32[5,4,2,1152]{3,1,2,0:T(4,128)S(1)} collective-permute-done((f32[5,4,2,1152]{3,1,2,0:T(4,128)S(1)}, f32[5,4,2,1152]{3,1,2,0:T(4,128)S(1)}, u32[]{:S(2)}, u32[]{:S(2)}) %collective-permute-start.2) | collective-permute-done | bytes 184352 | tf_op jit(solution)/shard_map/ppermute | solution.py:23
  41.2 0.6 broadcast_multiply_fusion.4
  43.5 8.0 %collective-permute-start.4 = (f32[5,4,2,1152]{3,1,2,0:T(4,128)S(1)}, f32[5,4,2,1152]{3,1,2,0:T(4,128)S(1)}, u32[]{:S(2)}, u32[]{:S(2)}) collective-permute-start(f32[5,4,2,1152]{3,1,2,0:T(4,128)S(1)} %copy.126), channel_id=1, source_target_pairs={{8,0},{16,8},{24,16},{32,24},{40,32},{48,40},{56,48},{64,56},{72,6... | collective-permute-start | bytes 552968 | tf_op jit(solution)/shard_map/ppermute | solution.py:23
  51.6 1.9 %collective-permute-start.5 = (f32[5,4,2,1152]{3,1,2,0:T(4,128)S(1)}, f32[5,4,2,1152]{3,1,2,0:T(4,128)S(1)}, u32[]{:S(2)}, u32[]{:S(2)}) collective-permute-start(f32[5,4,2,1152]{3,1,2,0:T(4,128)S(1)} %copy.127), channel_id=1, source_target_pairs={{0,8},{8,16},{16,24},{24,32},{32,40},{40,48},{48,56},{56,64},{64,7... | collective-permute-start | bytes 552968 | tf_op jit(solution)/shard_map/ppermute | solution.py:22
  53.6 1.0 collective-permute-done.4
  54.6 8.0 %collective-permute-done.5 = f32[5,4,2,1152]{3,1,2,0:T(4,128)S(1)} collective-permute-done((f32[5,4,2,1152]{3,1,2,0:T(4,128)S(1)}, f32[5,4,2,1152]{3,1,2,0:T(4,128)S(1)}, u32[]{:S(2)}, u32[]{:S(2)}) %collective-permute-start.5) | collective-permute-done | bytes 184352 | tf_op jit(solution)/shard_map/ppermute | solution.py:22
  62.7 0.6 broadcast_multiply_fusion.2
  65.0 1.9 %collective-permute-start.6 = (f32[5,4,2,1152]{3,1,2,0:T(4,128)S(1)}, f32[5,4,2,1152]{3,1,2,0:T(4,128)S(1)}, u32[]{:S(2)}, u32[]{:S(2)}) collective-permute-start(f32[5,4,2,1152]{3,1,2,0:T(4,128)S(1)} %copy.128), channel_id=1, source_target_pairs={{8,0},{16,8},{24,16},{32,24},{40,32},{48,40},{56,48},{64,56},{72,6... | collective-permute-start | bytes 552968 | tf_op jit(solution)/shard_map/ppermute | solution.py:23
  67.0 2.6 %collective-permute-start.7 = (f32[5,4,2,1152]{3,1,2,0:T(4,128)S(1)}, f32[5,4,2,1152]{3,1,2,0:T(4,128)S(1)}, u32[]{:S(2)}, u32[]{:S(2)}) collective-permute-start(f32[5,4,2,1152]{3,1,2,0:T(4,128)S(1)} %copy.129), channel_id=1, source_target_pairs={{0,8},{8,16},{16,24},{24,32},{32,40},{40,48},{48,56},{56,64},{64,7... | collective-permute-start | bytes 552968 | tf_op jit(solution)/shard_map/ppermute | solution.py:22
  70.1 8.0 %collective-permute-done.7 = f32[5,4,2,1152]{3,1,2,0:T(4,128)S(1)} collective-permute-done((f32[5,4,2,1152]{3,1,2,0:T(4,128)S(1)}, f32[5,4,2,1152]{3,1,2,0:T(4,128)S(1)}, u32[]{:S(2)}, u32[]{:S(2)}) %collective-permute-start.7) | collective-permute-done | bytes 184352 | tf_op jit(solution)/shard_map/ppermute | solution.py:22
  78.2 0.6 broadcast_multiply_fusion
  79.7 7.5 %copy.110 = f32[5,4,8,1152]{2,1,0,3:T(4,128)} copy(f32[5,4,8,1152]{3,2,1,0:T(8,128)S(1)} %fusion.39) | data formatting | bytes 1474560 | tf_op jit(solution)/shard_map/concatenate | solution.py:109
  87.2 15.3 %reshape.179 = f32[8,1,23040]{2,1,0:T(1,128)} reshape(f32[1152,5,4,8]{3,2,1,0:T(4,128)} %bitcast.193) | data formatting | bytes 1474560
  102.5 7.5 %all-to-all-start = ((f32[8,1,23040]{2,1,0:T(1,128)}), f32[8,1,23040]{2,1,0:T(1,128)S(1)}, u32[]{:S(2)}, u32[]{:S(2)}) async-start(f32[8,1,23040]{2,1,0:T(1,128)} %reshape.179), calls=%async_computation | async-start | bytes 1474560 | tf_op jit(solution)/shard_map/all_to_all | solution.py:110
  110.0 0.6 reduce_sum.9
  110.6 0.6 fusion.123
  111.7 1.2 broadcast_divide_fusion
  112.9 6.3 %all-to-all-done = f32[8,1,23040]{2,1,0:T(1,128)S(1)} async-done(((f32[8,1,23040]{2,1,0:T(1,128)}), f32[8,1,23040]{2,1,0:T(1,128)S(1)}, u32[]{:S(2)}, u32[]{:S(2)}) %all-to-all-start) | async-done | bytes 737312 | tf_op jit(solution)/shard_map/all_to_all | solution.py:110
  119.8 2.5 %reduce.8 = f32[8,23040]{1,0:T(8,128)S(1)} reduce(f32[8,1,23040]{2,1,0:T(1,128)S(1)} %all-to-all-done, f32[]{:T(128)} %broadcast.297), dimensions={1}, to_apply=%all_to_all.22.reduce_sub_computation | reduce | bytes 1474564 | tf_op jit(solution)/shard_map/all_to_all | solution.py:110
  122.2 18.2 %reshape.180 = f32[1152,5,4,8]{3,2,1,0:T(4,128)} reshape(f32[8,23040]{1,0:T(8,128)S(1)} %reduce.8) | data formatting | bytes 1474560
  140.4 9.4 %copy.111 = f32[5,4,8,8,144]{4,2,1,3,0:T(8,128)S(1)} copy(f32[5,4,8,8,144]{2,1,0,4,3:T(4,128)} %bitcast.194) | data formatting | bytes 1474560 | tf_op jit(solution)/shard_map/all_to_all | solution.py:110
  150.9 14.1 %while.14 = (s32[]{:T(128)}, f32[4,33,1152]{2,1,0:T(8,128)S(1)}, f32[4,32,1152]{2,1,0:T(8,128)S(1)}, f32[32,1152]{1,0:T(8,128)S(1)}, f32[32,1152]{1,0:T(8,128)S(...) while((s32[]{:T(128)}, f32[4,33,1152]{2,1,0:T(8,128)S(1)}, ...), condition=%wide.region_4.5_spmd.clone, body=%wide.region_3.4_spmd.clone.sunk | while | flops 608259 | bytes 1645299 | solution.py:82
  165.6 0.7 reshape.172
  167.4 17.3 %all_to_all.30 = f32[6,32,8,144]{3,2,0,1:T(8,128)S(1)} all-to-all(f32[6,32,8,144]{3,2,0,1:T(8,128)S(1)} %pad_maximum_fusion), channel_id=1, replica_groups=mesh['lat'=32,'lev'=8] {'lev'}, dimensions={1} | all-to-all | bytes 1769472 | tf_op jit(solution)/shard_map/all_to_all | solution.py:123
  185.0 0.6 copy.117
  185.7 1.2 slice.452
  187.0 0.8 squeeze.88
  188.0 0.8 squeeze.89
  (278 shorter events, 23.8 us)
Async XLA Ops:
  0.6 110.8 %copy-start = (f32[8,1152]{1,0:T(8,128)S(1)}, f32[8,1152]{1,0:T(8,128)}, u32[]{:S(2)}) copy-start(f32[8,1152]{1,0:T(8,128)} %param.12) | copy-start | bytes 110596
  1.6 0.7 copy-start.5
  4.3 8.8 %collective-permute-start = (f32[5,4,2,1152]{3,1,2,0:T(4,128)}, f32[5,4,2,1152]{3,1,2,0:T(4,128)}, u32[]{:S(2)}, u32[]{:S(2)}) collective-permute-start(f32[5,4,2,1152]{3,1,2,0:T(4,128)} %copy.122), channel_id=1, source_target_pairs={{8,0},{16,8},{24,16},{32,24},{40,32},{48,40},{56,48},{64,56},{72,6... | collective-permute-start | bytes 552968 | tf_op jit(solution)/shard_map/ppermute | solution.py:23
  8.2 13.3 %collective-permute-start.1 = (f32[5,4,2,1152]{3,1,2,0:T(4,128)}, f32[5,4,2,1152]{3,1,2,0:T(4,128)}, u32[]{:S(2)}, u32[]{:S(2)}) collective-permute-start(f32[5,4,2,1152]{3,1,2,0:T(4,128)} %copy.123), channel_id=1, source_target_pairs={{0,8},{8,16},{16,24},{24,32},{32,40},{40,48},{48,56},{56,64},{64,7... | collective-permute-start | bytes 552968 | tf_op jit(solution)/shard_map/ppermute | solution.py:22
  10.4 1.9 copy-start.1
  11.5 11.0 %copy-start.3 = (f32[4,8,1152]{2,1,0:T(8,128)S(1)}, f32[4,8,1152]{2,1,0:T(8,128)}, u32[]{:S(2)}) copy-start(f32[4,8,1152]{2,1,0:T(8,128)} %param.9) | copy-start | bytes 442372
  24.0 1.1 copy-start.2
  24.0 1.1 copy-start.6
  24.0 1.2 copy-start.7
  24.0 1.2 copy-start.9
  25.8 0.9 copy-start.4
  25.8 1.0 copy-start.8
  27.7 11.2 %collective-permute-start.3 = (f32[5,4,2,1152]{3,1,2,0:T(4,128)S(1)}, f32[5,4,2,1152]{3,1,2,0:T(4,128)S(1)}, u32[]{:S(2)}, u32[]{:S(2)}) collective-permute-start(f32[5,4,2,1152]{3,1,2,0:T(4,128)S(1)} %copy.125), channel_id=1, source_target_pairs={{0,8},{8,16},{16,24},{24,32},{32,40},{40,48},{48,56},{56,64},{64,7... | collective-permute-start | bytes 552968 | tf_op jit(solution)/shard_map/ppermute | solution.py:22
  29.6 11.4 %collective-permute-start.2 = (f32[5,4,2,1152]{3,1,2,0:T(4,128)S(1)}, f32[5,4,2,1152]{3,1,2,0:T(4,128)S(1)}, u32[]{:S(2)}, u32[]{:S(2)}) collective-permute-start(f32[5,4,2,1152]{3,1,2,0:T(4,128)S(1)} %copy.124), channel_id=1, source_target_pairs={{8,0},{16,8},{24,16},{32,24},{40,32},{48,40},{56,48},{64,56},{72,6... | collective-permute-start | bytes 552968 | tf_op jit(solution)/shard_map/ppermute | solution.py:23
  43.5 11.0 %collective-permute-start.4 = (f32[5,4,2,1152]{3,1,2,0:T(4,128)S(1)}, f32[5,4,2,1152]{3,1,2,0:T(4,128)S(1)}, u32[]{:S(2)}, u32[]{:S(2)}) collective-permute-start(f32[5,4,2,1152]{3,1,2,0:T(4,128)S(1)} %copy.126), channel_id=1, source_target_pairs={{8,0},{16,8},{24,16},{32,24},{40,32},{48,40},{56,48},{64,56},{72,6... | collective-permute-start | bytes 552968 | tf_op jit(solution)/shard_map/ppermute | solution.py:23
  51.6 11.1 %collective-permute-start.5 = (f32[5,4,2,1152]{3,1,2,0:T(4,128)S(1)}, f32[5,4,2,1152]{3,1,2,0:T(4,128)S(1)}, u32[]{:S(2)}, u32[]{:S(2)}) collective-permute-start(f32[5,4,2,1152]{3,1,2,0:T(4,128)S(1)} %copy.127), channel_id=1, source_target_pairs={{0,8},{8,16},{16,24},{24,32},{32,40},{40,48},{48,56},{56,64},{64,7... | collective-permute-start | bytes 552968 | tf_op jit(solution)/shard_map/ppermute | solution.py:22
  65.0 5.0 %collective-permute-start.6 = (f32[5,4,2,1152]{3,1,2,0:T(4,128)S(1)}, f32[5,4,2,1152]{3,1,2,0:T(4,128)S(1)}, u32[]{:S(2)}, u32[]{:S(2)}) collective-permute-start(f32[5,4,2,1152]{3,1,2,0:T(4,128)S(1)} %copy.128), channel_id=1, source_target_pairs={{8,0},{16,8},{24,16},{32,24},{40,32},{48,40},{56,48},{64,56},{72,6... | collective-permute-start | bytes 552968 | tf_op jit(solution)/shard_map/ppermute | solution.py:23
  67.0 11.1 %collective-permute-start.7 = (f32[5,4,2,1152]{3,1,2,0:T(4,128)S(1)}, f32[5,4,2,1152]{3,1,2,0:T(4,128)S(1)}, u32[]{:S(2)}, u32[]{:S(2)}) collective-permute-start(f32[5,4,2,1152]{3,1,2,0:T(4,128)S(1)} %copy.129), channel_id=1, source_target_pairs={{0,8},{8,16},{16,24},{24,32},{32,40},{40,48},{48,56},{56,64},{64,7... | collective-permute-start | bytes 552968 | tf_op jit(solution)/shard_map/ppermute | solution.py:22
  102.5 7.5 %copy-start.11 = (f32[32]{0:T(128)S(1)}, f32[32]{0:T(128)}, u32[]{:S(2)}) copy-start(f32[32]{0:T(128)} %param.13) | copy-start | bytes 388
  102.5 16.7 %all-to-all-start = ((f32[8,1,23040]{2,1,0:T(1,128)}), f32[8,1,23040]{2,1,0:T(1,128)S(1)}, u32[]{:S(2)}, u32[]{:S(2)}) async-start(f32[8,1,23040]{2,1,0:T(1,128)} %reshape.179), calls=%async_computation | async-start | bytes 1474560 | tf_op jit(solution)/shard_map/all_to_all | solution.py:110
  150.9 14.2 %copy-start.10 = (f32[32]{0:T(128)S(1)}, f32[32]{0:T(128)}, u32[]{:S(2)}) copy-start(f32[32]{0:T(128)} %broadcast_divide_fusion) | copy-start | bytes 388
where the time goes:
time: 190 us; the launch traced here: 189 us
  local copies, waits for them, and re-layouts  72.2 us (38%)
  starting transfers between devices  36.8 us (19%)
  waiting for transfers between devices  34.3 us (18%)
  other arithmetic  24.9 us (13%)
  blocking collectives  17.3 us (9%)
    unnamed x40, local copies, waits for them, and re-layouts  37.7 us
    ppermute x4, waiting for transfers between devices, with_halo(): before = lax.ppermute(last, axis, up)  24.6 us
    ppermute x4, starting transfers between devices, with_halo(): after = lax.ppermute(leading, axis, down)  21 us
    all_to_all x1, blocking collectives, shards(): lax.all_to_all(jnp.concatenate([remapped, new_thickness[None], heights[No...  17.3 us
    all_to_all x2, local copies, waits for them, and re-layouts, shards(): lax.all_to_all(advanced, 'lev', split_axis=3, concat_axis=1, tiled=True)  9.86 us
    ppermute x4, starting transfers between devices, with_halo(): before = lax.ppermute(last, axis, up)  8.34 us
    concatenate x1, local copies, waits for them, and re-layouts, shards(): jnp.concatenate([gridded_quantities[:4], jnp.exp(gridded_quantities[4:])]...  7.49 us
    all_to_all x1, starting transfers between devices, shards(): lax.all_to_all(advanced, 'lev', split_axis=3, concat_axis=1, tiled=True)  7.48 us
  transfers between devices with their start and end apart: 9, of which 8 were waited for; matrix products, arithmetic and copies ran while one was open for 4% of the time, Pallas kernels for 0%

commit v1 on v0

v1 whole, which is shorter than its diff:
```python
import functools
import math

import jax
import jax.numpy as jnp
from jax import lax
from jax.experimental import pallas as pl
from jax.experimental.pallas import tpu as pltpu
from jax.sharding import PartitionSpec as P

MESH = pl.DeviceIdType.MESH
SUBSTEPS = 4
ADVECT = 0.3 / 12.0
PRESS = 0.15 / 12.0
ROTATION_RATE = 0.3
TOP_PRESSURE = 1.0

ROWS = 8
LON = 1152
CHUNKS = 3
TILES = 3
WIDE = 128 * TILES
SENT = 2 * WIDE + 256
BACK = 3 * WIDE
PEERS = 8


def kernel(
    lat_size,
    vel_ref, temp_ref, tracer_ref, thick_ref, surf_ref, frac_ref,
    out_ref, out_thick_ref, out_geo_ref,
    band, uv_a, pq_a, s_a, uv_b, pq_b, s_b, turn, bound, share, surf,
    fwd, got, ret, back, result,
    local_sem, halo_send, halo_recv, fwd_send, fwd_recv, ret_send, ret_recv, out_sem,
):
    lat, lev = lax.axis_index("lat"), lax.axis_index("lev")
    north = lax.rem(lat + lat_size - 1, lat_size)
    south = lax.rem(lat + 1, lat_size)

    def peer(step):
        return lax.rem(lev + 1 + step, PEERS)

    parts = ((vel_ref, 0, 64), (temp_ref, 64, 32), (tracer_ref, 96, 32), (thick_ref, 128, 32))
    own = [
        pltpu.make_async_copy(ref, band.at[1, pl.ds(at, size)], local_sem.at[n])
        for n, (ref, at, size) in enumerate(parts)
    ]
    own.append(pltpu.make_async_copy(surf_ref, surf, local_sem.at[4]))
    for copy in own:
        copy.start()

    barrier = pltpu.get_barrier_semaphore()
    for row in (north, south):
        pl.semaphore_signal(barrier, inc=1, device_id=(row, lev), device_id_type=MESH)
    for step in range(PEERS - 1):
        pl.semaphore_signal(barrier, inc=1, device_id=(lat, peer(step)), device_id_type=MESH)
    pl.semaphore_wait(barrier, PEERS + 1)

    halo = [
        pltpu.make_async_remote_copy(
            src_ref=ref,
            dst_ref=band.at[where, pl.ds(at, size)],
            send_sem=halo_send.at[way, n],
            recv_sem=halo_recv.at[way, n],
            device_id=(row, lev),
            device_id_type=MESH,
        )
        for way, (row, where) in enumerate(((south, 0), (north, 2)))
        for n, (ref, at, size) in enumerate(parts)
    ]
    for copy in halo:
        copy.start()

    total = jnp.float32(0.0)
    for k in range(4 * PEERS):
        total = total + frac_ref[k]
        share[k, :] = jnp.full((128,), frac_ref[k], jnp.float32)
        bound[k, :] = jnp.full((128,), total, jnp.float32)
    share[...] = share[...] / total
    bound[...] = bound[...] / total

    sub = lax.broadcasted_iota(jnp.int32, (8, 128), 0)
    low = lax.broadcasted_iota(jnp.int32, (8, LON), 0) < 4
    row_of = lax.broadcasted_iota(jnp.int32, (3 * ROWS, 8, 128), 0) + (lat - 1) * ROWS
    angle = -0.5 * math.pi + (row_of.astype(jnp.float32) + 0.5) * (math.pi / (lat_size * ROWS))
    sign = jnp.where(lax.broadcasted_iota(jnp.int32, (3 * ROWS, 8, 128), 1) < 4, ROTATION_RATE, -ROTATION_RATE)
    turn[...] = sign * jnp.sin(angle)

    def inside(j):
        row = (lat - 1) * ROWS + j
        return jnp.where((row >= 0) & (row < lat_size * ROWS), 1.0, 0.0).astype(jnp.float32)

    def transposed(xs):
        for d in (4, 2, 1):
            ys = list(xs)
            for i in range(8):
                if not i & d:
                    ys[i] = jnp.where(sub & d == 0, xs[i], pltpu.roll(xs[i + d], d, 0))
                    ys[i + d] = jnp.where(sub & d == 0, pltpu.roll(xs[i], 8 - d, 0), xs[i + d])
            xs = ys
        return xs

    def unpack(b):
        keep = inside(b * ROWS)

        def body(t, carry):
            lanes = pl.ds(pl.multiple_of(t * 128, 128), 128)
            for dst, at in ((uv_a, 0), (pq_a, 64)):
                xs = [band[b, at + 8 * i : at + 8 * i + 8, lanes] * keep for i in range(8)]
                for r, x in enumerate(transposed(xs)):
                    dst[b * ROWS + r, :, lanes] = x
            xs = [jnp.log(band[b, 128 + 8 * i : 136 + 8 * i, lanes]) * keep for i in range(4)]
            for r, x in enumerate(transposed(xs + xs)):
                s_a[b * ROWS + r, :, lanes] = x
            return carry

        lax.fori_loop(0, LON // 128, body, 0)

    def east(a):
        return 8.0 * (pltpu.roll(a, LON - 1, 1) - pltpu.roll(a, 1, 1)) - (
            pltpu.roll(a, LON - 2, 1) - pltpu.roll(a, 2, 1)
        )

    def up(ref, j):
        return 8.0 * (ref[j + 1] - ref[j - 1]) - (ref[j + 2] - ref[j - 2])

    def advance(state, j):
        uv_ref, pq_ref, s_ref = state
        uv, pq, s = uv_ref[j], pq_ref[j], s_ref[j]
        turned = pltpu.roll(uv, 4, 0)
        eastward = jnp.where(low, uv, turned) * ADVECT
        northward = jnp.where(low, turned, uv) * ADVECT
        new_pq = pq - eastward * east(pq) - northward * up(pq_ref, j)
        s_east, s_up = east(s), up(s_ref, j)
        uv_east, uv_up = east(uv), up(uv_ref, j)
        spin = jnp.concatenate([turn[j]] * (LON // 128), axis=1)
        new_uv = uv - eastward * uv_east - northward * uv_up - PRESS * jnp.where(low, s_east, s_up) + spin * turned
        spread = jnp.where(low, uv_east, uv_up)
        new_s = s - eastward * s_east - northward * s_up - ADVECT * (spread + pltpu.roll(spread, 4, 0))
        return new_uv, new_pq, new_s

    def substep(src, dst, first, last):
        def body(j, carry):
            keep = inside(j)
            new_uv, new_pq, new_s = advance(src, j)
            dst[0][j] = new_uv * keep
            dst[1][j] = new_pq
            dst[2][j] = new_s * keep
            return carry

        lax.fori_loop(first, last, body, 0)

    a, b = (uv_a, pq_a, s_a), (uv_b, pq_b, s_b)
    for copy in own:
        copy.wait()
    unpack(1)
    substep(a, b, 10, 14)
    for copy in halo[:4]:
        copy.wait()
    unpack(0)
    substep(a, b, 2, 10)
    for copy in halo[4:]:
        copy.wait()
    unpack(2)
    substep(a, b, 14, 22)
    substep(b, a, 4, 20)
    substep(a, b, 6, 18)

    def message(r, put):
        new_uv, new_pq, new_s = advance(b, ROWS + r)
        for c in range(CHUNKS):
            at = c * WIDE
            put(c, slice(0, WIDE), new_uv[:, at : at + WIDE])
            put(c, slice(WIDE, 2 * WIDE), new_pq[:, at : at + WIDE])
            s0, s1, s2 = (new_s[:, at + 128 * t : at + 128 * (t + 1)] for t in range(TILES))
            put(c, slice(2 * WIDE, 2 * WIDE + 128), jnp.where(sub < 4, s0, s2))
            put(c, slice(2 * WIDE + 128, SENT), s1)

    def fwd_copy(c, step):
        return pltpu.make_async_remote_copy(
            src_ref=fwd.at[c, step],
            dst_ref=got.at[c, lev],
            send_sem=fwd_send.at[c, step],
            recv_sem=fwd_recv.at[c, step],
            device_id=(lat, peer(step)),
            device_id_type=MESH,
        )

    def last_row(step, carry):
        def put(c, lanes, value):
            fwd[c, step, :, lanes] = value

        message(peer(step), put)
        fwd_copy(0, step).start()
        return carry

    lax.fori_loop(0, PEERS - 1, last_row, 0)
    for c in range(1, CHUNKS):
        lax.fori_loop(0, PEERS - 1, lambda k, z, c=c: (fwd_copy(c, k).start(), z)[1], 0)

    def put_own(c, lanes, value):
        got[c, lev, :, lanes] = value

    message(lev, put_own)

    def ret_copy(c, step):
        return pltpu.make_async_remote_copy(
            src_ref=ret.at[c, peer(step)],
            dst_ref=back.at[c, lev],
            send_sem=ret_send.at[c, step],
            recv_sem=ret_recv.at[c, step],
            device_id=(lat, peer(step)),
            device_id_type=MESH,
        )

    small = sub < 4

    def flip(x):
        return pltpu.roll(x, 4, 0)

    def running(values):
        out, carry = [], None
        for v in values:
            for d in (1, 2, 4):
                v = v + jnp.where(sub >= d, pltpu.roll(v, d, 0), 0.0)
            if carry is not None:
                v = v + carry
            out.append(v)
            carry = v[7:8]
        return out

    def previous(values):
        out, carry = [], jnp.zeros((1, 128), jnp.float32)
        for v in values:
            out.append(jnp.where(sub == 0, carry, pltpu.roll(v, 1, 0)))
            carry = v[7:8]
        return out

    def gather(x, index):
        return jnp.take_along_axis(x, index, axis=0, mode="promise_in_bounds")

    def tile(c, t):
        at = pl.multiple_of(t * 128, 128)

        def split(start):
            xs = [got[c, p, :, pl.ds(start + at, 128)] for p in range(PEERS)]
            first = [jnp.where(small, xs[2 * i], flip(xs[2 * i + 1])) for i in range(4)]
            second = [jnp.where(small, flip(xs[2 * i]), xs[2 * i + 1]) for i in range(4)]
            return first, second

        u, v = split(0)
        temp, tracer = split(WIDE)
        high = t == 2
        s_at = pl.multiple_of(2 * WIDE + jnp.where(high, 0, t) * 128, 128)
        xs = [got[c, p, :, pl.ds(s_at, 128)] for p in range(PEERS)]
        layer = []
        for i in range(4):
            lower_half = jnp.where(small, xs[2 * i], flip(xs[2 * i + 1]))
            upper_half = jnp.where(small, flip(xs[2 * i]), xs[2 * i + 1])
            layer.append(jnp.exp(jnp.where(high, upper_half, lower_half)))
        lower = running(layer)
        upper = [x - y for x, y in zip(lower, layer)]
        bottom = lower[3][7:8]
        fields = (u, v, temp, tracer)
        before = []
        for f in fields:
            weighted = [x * y for x, y in zip(f, layer)]
            before.append([x - y for x, y in zip(running(weighted), weighted)])
        target = [bottom * bound[8 * i : 8 * i + 8, :] for i in range(4)]
        integral = [[] for _ in fields]
        ends = [lower[m][7:8] for m in range(3)]
        mids = [jnp.broadcast_to(lower[m][3:4], (8, 128)) for m in range(4)]
        for i in range(4):
            goal = target[i]
            past = [goal > e for e in ends]

            def pick(q):
                return jnp.where(past[2], q[3], jnp.where(past[1], q[2], jnp.where(past[0], q[1], q[0])))

            pos = jnp.where(pick(mids) < goal, 4, 0)
            pos = pos + jnp.where(pick([gather(x, pos + 1) for x in lower]) < goal, 2, 0)
            pos = pos + jnp.where(pick([gather(x, pos) for x in lower]) < goal, 1, 0)

            def here(q):
                return pick([gather(x, pos) for x in q])

            depth = goal - here(upper)
            for n, f in enumerate(fields):
                integral[n].append(here(before[n]) + depth * here(f))
        new_thick = [bottom * share[8 * i : 8 * i + 8, :] for i in range(4)]
        inverse = [1.0 / x for x in new_thick]
        remapped = [[(x - y) * z for x, y, z in zip(g, previous(g), inverse)] for g in integral]
        rise = [
            r * jnp.log((TOP_PRESSURE + x) / (TOP_PRESSURE + y))
            for r, x, y in zip(remapped[2], target, previous(target))
        ]
        geo = [None] * 4
        ground = surf[:, pl.ds(pl.multiple_of(c * WIDE + t * 128, 128), 128)]
        carry = jnp.sum(jnp.where(sub == lev, ground, 0.0), axis=0, keepdims=True)
        for i in (3, 2, 1, 0):
            x = rise[i]
            for d in (1, 2, 4):
                x = x + jnp.where(sub < 8 - d, pltpu.roll(x, 8 - d, 0), 0.0)
            geo[i] = x + carry
            carry = geo[i][0:1]
        for start, (one, two) in (
            (0, (remapped[0], remapped[1])),
            (WIDE, (remapped[2], remapped[3])),
            (2 * WIDE, (geo, new_thick)),
        ):
            for i in range(4):
                ret[c, 2 * i, :, pl.ds(start + at, 128)] = jnp.where(small, one[i], flip(two[i]))
                ret[c, 2 * i + 1, :, pl.ds(start + at, 128)] = jnp.where(small, flip(one[i]), two[i])

    def chunk(c, carry):
        lax.fori_loop(0, PEERS - 1, lambda k, z: (fwd_copy(c, k).wait_recv(), z)[1], 0)
        lax.fori_loop(0, TILES, lambda t, z: (tile(c, t), z)[1], 0)
        lax.fori_loop(0, PEERS - 1, lambda k, z: (ret_copy(c, k).start(), z)[1], 0)
        return carry

    lax.fori_loop(0, CHUNKS, chunk, 0)

    def deliver(c, carry):
        lax.fori_loop(0, PEERS - 1, lambda k, z: (ret_copy(c, k).wait_recv(), z)[1], 0)
        lax.fori_loop(0, PEERS - 1, lambda k, z: (ret_copy(c, k).wait_send(), z)[1], 0)
        back[c, lev] = ret[c, lev]

        def body(t, carry):
            at = pl.multiple_of(t * 128, 128)
            lanes = pl.ds(pl.multiple_of(c * WIDE + t * 128, 128), 128)
            for n in range(3):
                xs = [back[c, r, :, pl.ds(n * WIDE + at, 128)] for r in range(ROWS)]
                for i, x in enumerate(transposed(xs)):
                    result[64 * n + 8 * i : 64 * n + 8 * i + 8, lanes] = x
            return carry

        lax.fori_loop(0, TILES, body, 0)
        return carry

    lax.fori_loop(0, CHUNKS, deliver, 0)

    outs = [
        pltpu.make_async_copy(result.at[pl.ds(at, size)], ref, out_sem.at[n])
        for n, (ref, at, size) in enumerate(((out_ref, 0, 128), (out_geo_ref, 128, 32), (out_thick_ref, 160, 32)))
    ]
    for copy in outs:
        copy.start()

    def sent(n, carry):
        c, step = n // (PEERS - 1), lax.rem(n, PEERS - 1)
        fwd_copy(c, step).wait_send()
        return carry

    lax.fori_loop(0, CHUNKS * (PEERS - 1), sent, 0)
    for copy in outs:
        copy.wait()


def shards(lat_size, velocity, potential_temp, tracer, thickness, surface_height, level_fractions):
    anywhere = pl.BlockSpec(memory_space=pl.ANY)
    f32 = jnp.float32
    state = [pltpu.VMEM((3 * ROWS, 8, LON), f32)] * 6
    remapped, new_thickness, geopotential = pl.pallas_call(
        functools.partial(kernel, lat_size),
        out_shape=(
            jax.ShapeDtypeStruct((128, LON), f32),
            jax.ShapeDtypeStruct((32, LON), f32),
            jax.ShapeDtypeStruct((32, LON), f32),
        ),
        in_specs=[anywhere] * 5 + [pl.BlockSpec(memory_space=pltpu.SMEM)],
        out_specs=(anywhere,) * 3,
        scratch_shapes=[
            pltpu.VMEM((3, 160, LON), f32),
            *state,
            pltpu.VMEM((3 * ROWS, 8, 128), f32),
            pltpu.VMEM((32, 128), f32),
            pltpu.VMEM((32, 128), f32),
            pltpu.VMEM((ROWS, LON), f32),
            pltpu.VMEM((CHUNKS, PEERS - 1, 8, SENT), f32),
            pltpu.VMEM((CHUNKS, PEERS, 8, SENT), f32),
            pltpu.VMEM((CHUNKS, PEERS, 8, BACK), f32),
            pltpu.VMEM((CHUNKS, PEERS, 8, BACK), f32),
            pltpu.VMEM((192, LON), f32),
            pltpu.SemaphoreType.DMA((5,)),
            pltpu.SemaphoreType.DMA((2, 4)),
            pltpu.SemaphoreType.DMA((2, 4)),
            pltpu.SemaphoreType.DMA((CHUNKS, PEERS - 1)),
            pltpu.SemaphoreType.DMA((CHUNKS, PEERS - 1)),
            pltpu.SemaphoreType.DMA((CHUNKS, PEERS - 1)),
            pltpu.SemaphoreType.DMA((CHUNKS, PEERS - 1)),
            pltpu.SemaphoreType.DMA((3,)),
        ],
        compiler_params=pltpu.CompilerParams(
            collective_id=0, has_side_effects=True, vmem_limit_bytes=40 * 2**20
        ),
        cost_estimate=pl.CostEstimate(flops=10**8, bytes_accessed=2 * 10**6, transcendentals=10**6),
    )(
        velocity.reshape(64, LON),
        potential_temp.reshape(32, LON),
        tracer.reshape(32, LON),
        thickness.reshape(32, LON),
        surface_height,
        level_fractions,
    )
    return (
        remapped.reshape(4, 4, ROWS, LON),
        new_thickness.reshape(4, ROWS, LON),
        geopotential.reshape(4, ROWS, LON),
    )


def solution(mesh):
    return jax.shard_map(
        functools.partial(shards, mesh.shape["lat"]),
        mesh=mesh,
        in_specs=(
            P(None, "lev", "lat", None),
            P("lev", "lat", None),
            P("lev", "lat", None),
            P("lev", "lat", None),
            P("lat", None),
            P(),
        ),
        out_specs=(P(None, "lev", "lat", None), P("lev", "lat", None), P("lev", "lat", None)),
        check_vma=False,
    )
```

time: 190 us -> 63.4 us (0.33)
  the two profiles are of different devices: /device:TPU:128 before, /device:TPU:8 now
where the time goes in v1:
time: 63.4 us; the launch traced here: 63.1 us
  Pallas kernels  55.2 us (87%)
  local copies, waits for them, and re-layouts  7.24 us (11%)
  between operations  0.65 us (1%)
    pallas_call x1, Pallas kernels, shards(): pl.pallas_call(functools.partial(kernel, lat_size), out_shape=(jax.ShapeD...  55.2 us
    unnamed x15, local copies, waits for them, and re-layouts  7.24 us

profile of v1, /device:TPU:8, one launch (start us, length us, event | category | flops | bytes accessed | tf_op | source)
XLA Modules:
  0.0 63.1 jit_solution(4423474532465947996)
XLA Ops:
  0.6 0.0 copy-start.5
  0.6 0.6 %copy-done.5 = f32[32]{0:T(128)S(1)} copy-done((f32[32]{0:T(128)S(1)}, f32[32]{0:T(128)}, u32[]{:S(2)}) %copy-start.5) | copy-done | bytes 152
  1.3 0.0 copy-start
  1.3 1.0 %copy-done = f32[2,4,8,1152]{3,2,1,0:T(8,128)S(1)} copy-done((f32[2,4,8,1152]{3,2,1,0:T(8,128)S(1)}, f32[2,4,8,1152]{3,2,1,0:T(8,128)}, u32[]{:S(2)}) %copy-start) | copy-done | bytes 294936
  2.3 0.0 copy-start.1
  2.3 0.9 %copy-done.1 = f32[4,8,1152]{2,1,0:T(8,128)S(1)} copy-done((f32[4,8,1152]{2,1,0:T(8,128)S(1)}, f32[4,8,1152]{2,1,0:T(8,128)}, u32[]{:S(2)}) %copy-start.1) | copy-done | bytes 147480
  3.2 0.0 copy-start.2
  3.2 0.9 %copy-done.2 = f32[4,8,1152]{2,1,0:T(8,128)S(1)} copy-done((f32[4,8,1152]{2,1,0:T(8,128)S(1)}, f32[4,8,1152]{2,1,0:T(8,128)}, u32[]{:S(2)}) %copy-start.2) | copy-done | bytes 147480
  4.1 0.0 copy-start.3
  4.1 0.9 %copy-done.3 = f32[4,8,1152]{2,1,0:T(8,128)S(1)} copy-done((f32[4,8,1152]{2,1,0:T(8,128)S(1)}, f32[4,8,1152]{2,1,0:T(8,128)}, u32[]{:S(2)}) %copy-start.3) | copy-done | bytes 147480
  5.0 0.0 copy-start.4
  5.0 0.8 %copy-done.4 = f32[8,1152]{1,0:T(8,128)S(1)} copy-done((f32[8,1152]{1,0:T(8,128)S(1)}, f32[8,1152]{1,0:T(8,128)}, u32[]{:S(2)}) %copy-start.4) | copy-done | bytes 36888
  5.8 55.2 %shard_map.85 = (f32[128,1152]{1,0:T(8,128)S(1)}, f32[32,1152]{1,0:T(8,128)S(1)}, f32[32,1152]{1,0:T(8,128)S(1)}) custom-call(f32[64,1152]{1,0:T(8,128)S(1)} %bitcast.10, f32[32,1152]{1,0:T(8,128)S(1)} %bitcast.11, f32[32,1152]{1,0:T(8,128)S(1)} %bitcast.12, f32[32,1152]{1,0:T(8,128)S(1)} %bitcast.13, f32[8,1152]{1,0:T(8,128)S(1)} %copy-done.4, f32[32]{0:T(128)S(1)} %copy-done.5), custom_call_target="tpu_custom_call" | custom-call | flops 100000000 | bytes 2000000 | tf_op jit(solution)/shard_map/pallas_call | solution.py:363
  61.0 0.8 %copy.12 = f32[4,4,8,1152]{3,2,1,0:T(8,128)} copy(f32[4,4,8,1152]{3,2,1,0:T(8,128)S(1)} %bitcast.7) | data formatting | bytes 1179648
  61.8 0.7 %copy.13 = f32[4,8,1152]{2,1,0:T(8,128)} copy(f32[4,8,1152]{2,1,0:T(8,128)S(1)} %bitcast.9) | data formatting | bytes 294912
  62.5 0.7 %copy.14 = f32[4,8,1152]{2,1,0:T(8,128)} copy(f32[4,8,1152]{2,1,0:T(8,128)S(1)} %bitcast.8) | data formatting | bytes 294912
Async XLA Ops:
  0.6 0.7 %copy-start.5 = (f32[32]{0:T(128)S(1)}, f32[32]{0:T(128)}, u32[]{:S(2)}) copy-start(f32[32]{0:T(128)} %frac_ref.1) | copy-start | bytes 388
  1.3 1.0 %copy-start = (f32[2,4,8,1152]{3,2,1,0:T(8,128)S(1)}, f32[2,4,8,1152]{3,2,1,0:T(8,128)}, u32[]{:S(2)}) copy-start(f32[2,4,8,1152]{3,2,1,0:T(8,128)} %param.6) | copy-start | bytes 884740
  2.3 0.9 %copy-start.1 = (f32[4,8,1152]{2,1,0:T(8,128)S(1)}, f32[4,8,1152]{2,1,0:T(8,128)}, u32[]{:S(2)}) copy-start(f32[4,8,1152]{2,1,0:T(8,128)} %param.7) | copy-start | bytes 442372
  3.2 0.9 %copy-start.2 = (f32[4,8,1152]{2,1,0:T(8,128)S(1)}, f32[4,8,1152]{2,1,0:T(8,128)}, u32[]{:S(2)}) copy-start(f32[4,8,1152]{2,1,0:T(8,128)} %param.8) | copy-start | bytes 442372
  4.1 0.9 %copy-start.3 = (f32[4,8,1152]{2,1,0:T(8,128)S(1)}, f32[4,8,1152]{2,1,0:T(8,128)}, u32[]{:S(2)}) copy-start(f32[4,8,1152]{2,1,0:T(8,128)} %param.9) | copy-start | bytes 442372
  5.0 0.8 %copy-start.4 = (f32[8,1152]{1,0:T(8,128)S(1)}, f32[8,1152]{1,0:T(8,128)}, u32[]{:S(2)}) copy-start(f32[8,1152]{1,0:T(8,128)} %surf_ref.1) | copy-start | bytes 110596

commit v2 on v1

v2 whole, which is shorter than its diff:
```python
import functools
import math

import jax
import jax.numpy as jnp
from jax import lax
from jax.experimental import pallas as pl
from jax.experimental.pallas import tpu as pltpu
from jax.sharding import PartitionSpec as P

MESH = pl.DeviceIdType.MESH
SUBSTEPS = 4
ADVECT = 0.3 / 12.0
PRESS = 0.15 / 12.0
ROTATION_RATE = 0.3
TOP_PRESSURE = 1.0

ROWS = 8
LON = 1152
TILES = 9
ROW = 2 * LON + 640
PIECE = 384
PEERS = 8
RING = 8


def kernel(
    lat_size,
    vel_ref, temp_ref, tracer_ref, thick_ref, surf_ref, frac_ref,
    out_ref, out_thick_ref, out_geo_ref,
    frac, band, rows, s_0, uv_1, pq_1, s_1, uv_2, pq_2, s_2, uv_3, pq_3, s_3, turn, bound, share, surf,
    relay, fwd, got, ret, back, result,
    local_sem, halo_send, halo_recv, relay_send, relay_recv, fwd_send, fwd_recv, ret_send, ret_recv, out_sem,
):
    lat, lev = lax.axis_index("lat"), lax.axis_index("lev")
    relayed = lat_size % RING == 0 and lat_size > RING

    def band_at(offset):
        return lax.rem(lat + offset + lat_size, lat_size)

    def lane(t):
        return slice(128 * t, 128 * t + 128)

    parts = ((vel_ref, 0, 64), (temp_ref, 64, 32), (tracer_ref, 96, 32), (thick_ref, 128, 32))
    own = [
        pltpu.make_async_copy(ref, band.at[pl.ds(at, size)], local_sem.at[n])
        for n, (ref, at, size) in enumerate(parts)
    ]
    later = [
        pltpu.make_async_copy(surf_ref, surf, local_sem.at[4]),
        pltpu.make_async_copy(frac_ref, frac, local_sem.at[5]),
    ]
    for copy in own + later:
        copy.start()

    has_north, has_south = lat > 0, lat < lat_size - 1
    before_step = lax.rem(lat, RING) == RING - 1
    after_step = lax.rem(lat, RING) == 0
    beside = band_at(jnp.where(before_step, 1 - RING, RING - 1))
    ahead, behind = lat + RING < lat_size, lat >= RING
    relays_south = after_step & ahead
    relays_north = before_step & behind

    barrier = pltpu.get_barrier_semaphore()

    def greet(row):
        pl.semaphore_signal(barrier, inc=1, device_id=(row, lev), device_id_type=MESH)

    def peer(step):
        return lax.rem(lev + 1 + step, PEERS)

    pl.when(has_north)(lambda: greet(band_at(-1)))
    pl.when(has_south)(lambda: greet(band_at(1)))
    for step in range(PEERS - 1):
        pl.semaphore_signal(barrier, inc=1, device_id=(lat, peer(step)), device_id_type=MESH)
    guests = PEERS - 1 + jnp.where(has_north, 1, 0) + jnp.where(has_south, 1, 0)
    if relayed:

        @pl.when(before_step | after_step)
        def _():
            greet(beside)
            pl.when(ahead)(lambda: greet(band_at(RING)))
            pl.when(behind)(lambda: greet(band_at(-RING)))

        more = 1 + jnp.where(ahead, 1, 0) + jnp.where(behind, 1, 0)
        guests = guests + jnp.where(before_step | after_step, more, 0)

    sub = lax.broadcasted_iota(jnp.int32, (8, 128), 0)
    lanes_in = lax.broadcasted_iota(jnp.int32, (8, 128), 1)
    small = sub < 4

    def flip(x):
        return pltpu.roll(x, 4, 0)

    def transposed(xs):
        for d in (4, 2, 1):
            ys = list(xs)
            for i in range(8):
                if not i & d:
                    ys[i] = jnp.where(sub & d == 0, xs[i], pltpu.roll(xs[i + d], d, 0))
                    ys[i + d] = jnp.where(sub & d == 0, pltpu.roll(xs[i], 8 - d, 0), xs[i + d])
            xs = ys
        return xs

    for copy in own:
        copy.wait()

    def unpack(t, carry):
        at = pl.multiple_of(t * 128, 128)
        for start, n in ((0, 0), (LON, 64)):
            xs = [band[n + 8 * i : n + 8 * i + 8, pl.ds(at, 128)] for i in range(8)]
            for r, x in enumerate(transposed(xs)):
                rows[ROWS + r, :, pl.ds(start + at, 128)] = x
        xs = [jnp.log(band[128 + 8 * i : 136 + 8 * i, pl.ds(at, 128)]) for i in range(4)]
        for r, x in enumerate(transposed(xs + xs)):
            s_0[ROWS + r, :, pl.ds(at, 128)] = x
        return carry

    lax.fori_loop(0, TILES, unpack, 0)

    def fold(r, carry):
        j = ROWS + r
        for t in range(4):
            x = jnp.where(small, s_0[j, :, lane(t)], s_0[j, :, lane(t + 5)])
            rows[j, :, 2 * LON + 128 * t : 2 * LON + 128 * (t + 1)] = x
        rows[j, :, 2 * LON + 512 :] = s_0[j, :, lane(4)]
        return carry

    lax.fori_loop(0, ROWS, fold, 0)

    pl.semaphore_wait(barrier, guests)

    def remote(src, dst, send, recv, to):
        return pltpu.make_async_remote_copy(
            src_ref=src, dst_ref=dst, send_sem=send, recv_sem=recv, device_id=to, device_id_type=MESH
        )

    def to_south(h, src=None, row=None, send=None):
        return remote(
            rows.at[2 * ROWS - h] if src is None else src,
            rows.at[ROWS - h],
            halo_send.at[0, h - 1] if send is None else send,
            halo_recv.at[0, h - 1],
            (band_at(1) if row is None else row, lev),
        )

    def to_north(h, src=None, row=None, send=None):
        return remote(
            rows.at[ROWS - 1 + h] if src is None else src,
            rows.at[2 * ROWS - 1 + h],
            halo_send.at[1, h - 1] if send is None else send,
            halo_recv.at[1, h - 1],
            (band_at(-1) if row is None else row, lev),
        )

    def to_relay(way, h):
        n = h // 2 - 1
        src = rows.at[2 * ROWS - h] if way == 0 else rows.at[ROWS - 1 + h]
        return remote(src, relay.at[n], halo_send.at[way, h - 1], relay_recv.at[n], (beside, lev))

    for h in range(1, ROWS + 1):
        if relayed and h % 2 == 0:
            pl.when(has_south & before_step)(lambda h=h: to_relay(0, h).start())
            pl.when(has_south & jnp.logical_not(before_step))(lambda h=h: to_south(h).start())
            pl.when(has_north & after_step)(lambda h=h: to_relay(1, h).start())
            pl.when(has_north & jnp.logical_not(after_step))(lambda h=h: to_north(h).start())
        else:
            pl.when(has_south)(lambda h=h: to_south(h).start())
            pl.when(has_north)(lambda h=h: to_north(h).start())

    def forward_south(h):
        return to_south(h, relay.at[h // 2 - 1], band_at(RING), relay_send.at[h // 2 - 1])

    def forward_north(h):
        return to_north(h, relay.at[h // 2 - 1], band_at(-RING), relay_send.at[h // 2 - 1])

    def pass_on(h):
        @pl.when(relays_south)
        def _():
            to_relay(0, h).wait_recv()
            forward_south(h).start()

        @pl.when(relays_north)
        def _():
            to_relay(1, h).wait_recv()
            forward_north(h).start()

    for copy in later:
        copy.wait()
    total = jnp.float32(0.0)
    for k in range(4 * PEERS):
        total = total + frac[k]
        share[k, :] = jnp.full((128,), frac[k], jnp.float32)
        bound[k, :] = jnp.full((128,), total, jnp.float32)
    share[...] = share[...] / total
    bound[...] = bound[...] / total
    row_of = lax.broadcasted_iota(jnp.int32, (3 * ROWS, 8, 128), 0) + (lat - 1) * ROWS
    angle = -0.5 * math.pi + (row_of.astype(jnp.float32) + 0.5) * (math.pi / (lat_size * ROWS))
    sign = jnp.where(lax.broadcasted_iota(jnp.int32, (3 * ROWS, 8, 128), 1) < 4, ROTATION_RATE, -ROTATION_RATE)
    turn[...] = sign * jnp.sin(angle)

    def inside(j):
        row = (lat - 1) * ROWS + j
        return jnp.where((row >= 0) & (row < lat_size * ROWS), 1.0, 0.0).astype(jnp.float32)

    def advance(state, js, emits):
        (uv_ref, _), (pq_ref, pq_at), (s_ref, _) = state
        fields = ((uv_ref, 0), (pq_ref, pq_at), (s_ref, 0))

        def line(j, emit):
            spin = turn[j]

            def load(n, row, t):
                ref, at = fields[n]
                return ref[row, :, at + 128 * t : at + 128 * (t + 1)]

            here, rolled = {}, {}

            def value(n, t):
                if (n, t) not in here:
                    here[n, t] = load(n, j, t)
                return here[n, t]

            def roll(n, t, k):
                t = t % TILES
                if (n, t, k) not in rolled:
                    rolled[n, t, k] = pltpu.roll(value(n, t), k, 1)
                return rolled[n, t, k]

            def east(n, t):
                one = jnp.where(lanes_in < 127, roll(n, t, 127), roll(n, t + 1, 127)) - jnp.where(
                    lanes_in < 1, roll(n, t - 1, 1), roll(n, t, 1)
                )
                two = jnp.where(lanes_in < 126, roll(n, t, 126), roll(n, t + 1, 126)) - jnp.where(
                    lanes_in < 2, roll(n, t - 1, 2), roll(n, t, 2)
                )
                return 8.0 * one - two

            def up(n, t):
                return 8.0 * (load(n, j + 1, t) - load(n, j - 1, t)) - (load(n, j + 2, t) - load(n, j - 2, t))

            def step(t):
                uv, pq, s = (value(n, t) for n in range(3))
                turned = flip(uv)
                eastward = jnp.where(small, uv, turned) * ADVECT
                northward = jnp.where(small, turned, uv) * ADVECT
                uv_east, uv_up = east(0, t), up(0, t)
                s_east, s_up = east(2, t), up(2, t)
                new_pq = pq - eastward * east(1, t) - northward * up(1, t)
                push = PRESS * jnp.where(small, s_east, s_up)
                new_uv = uv - eastward * uv_east - northward * uv_up - push + spin * turned
                spread = jnp.where(small, uv_east, uv_up)
                new_s = s - eastward * s_east - northward * s_up - ADVECT * (spread + flip(spread))
                emit(t, new_uv, new_pq, new_s)

            return step

        steps = [line(j, emit) for j, emit in zip(js, emits)]
        for t in range(TILES):
            for step in steps:
                step(t)

    states = (
        ((rows, 0), (rows, LON), (s_0, 0)),
        ((uv_1, 0), (pq_1, 0), (s_1, 0)),
        ((uv_2, 0), (pq_2, 0), (s_2, 0)),
        ((uv_3, 0), (pq_3, 0), (s_3, 0)),
    )

    def substep(n, *js):
        dst = states[n]

        def into(j):
            keep = inside(j)

            def emit(t, new_uv, new_pq, new_s):
                dst[0][0][j, :, lane(t)] = new_uv * keep
                dst[1][0][j, :, lane(t)] = new_pq
                dst[2][0][j, :, lane(t)] = new_s * keep

            return emit

        advance(states[n - 1], js, [into(j) for j in js])

    def receive(way, h):
        j = ROWS - h if way == 0 else 2 * ROWS - 1 + h
        there = has_north if way == 0 else has_south
        pl.when(there)(lambda: (to_south(h) if way == 0 else to_north(h)).wait_recv())

        @pl.when(jnp.logical_not(there))
        def _():
            rows[j] = jnp.zeros((8, ROW), jnp.float32)

        for t in range(5):
            x = rows[j, :, 2 * LON + 128 * t : 2 * LON + 128 * (t + 1)]
            y = flip(x)
            s_0[j, :, lane(t)] = jnp.where(small, x, y)
            if t < 4:
                s_0[j, :, lane(t + 5)] = jnp.where(small, y, x)

    def fwd_copy(r, step):
        t = lax.rem(peer(step) - r + PEERS, PEERS)
        return remote(
            fwd.at[r, t], got.at[r, lev], fwd_send.at[r, step], fwd_recv.at[r, step], (lat, peer(step))
        )

    def extra_copy(r):
        step = lax.rem(r - lev - 1 + 2 * PEERS, PEERS)
        return remote(fwd.at[r, 8], got.at[8, lev], fwd_send.at[8, step], fwd_recv.at[8, step], (lat, r))

    def release(*rs):
        def into(r):
            def emit(t, new_uv, new_pq, new_s):
                fwd[r, t, :, lane(0)] = new_uv
                fwd[r, t, :, lane(1)] = new_pq
                fwd[r, t, :, lane(2)] = new_s

            return emit

        advance(states[3], [ROWS + r for r in rs], [into(r) for r in rs])
        for r in rs:
            lax.fori_loop(0, PEERS - 1, lambda k, z, r=r: (fwd_copy(r, k).start(), z)[1], 0)
            pl.when(r != lev)(lambda r=r: extra_copy(r).start())
            got[r, lev] = fwd[r, lax.rem(lev - r + PEERS, PEERS)]

            @pl.when(r == lev)
            def _(r=r):
                got[8, lev] = fwd[r, 8]

    def ret_copy(u, row, t, step):
        return remote(
            ret.at[u, peer(step)], back.at[t, row], ret_send.at[u, step], ret_recv.at[u, step], (lat, peer(step))
        )

    def running(values):
        out, carry = [], None
        for v in values:
            for d in (1, 2, 4):
                v = v + jnp.where(sub >= d, pltpu.roll(v, d, 0), 0.0)
            if carry is not None:
                v = v + carry
            out.append(v)
            carry = v[7:8]
        return out

    def previous(values):
        out, carry = [], jnp.zeros((1, 128), jnp.float32)
        for v in values:
            out.append(jnp.where(sub == 0, carry, pltpu.roll(v, 1, 0)))
            carry = v[7:8]
        return out

    def gather(x, index):
        return jnp.take_along_axis(x, index, axis=0, mode="promise_in_bounds")

    def remap(u):
        row = jnp.where(u < 8, u, lev)
        t = jnp.where(u < 8, lax.rem(lev - u + 2 * PEERS, PEERS), 8)
        lax.fori_loop(
            0,
            PEERS - 1,
            lambda k, z: (
                remote(
                    fwd.at[0, 0], got.at[u, lev], fwd_send.at[u, k], fwd_recv.at[u, k], (lat, peer(k))
                ).wait_recv(),
                z,
            )[1],
            0,
        )

        def split(n):
            xs = [got[u, p, :, lane(n)] for p in range(PEERS)]
            first = [jnp.where(small, xs[2 * i], flip(xs[2 * i + 1])) for i in range(4)]
            second = [jnp.where(small, flip(xs[2 * i]), xs[2 * i + 1]) for i in range(4)]
            return first, second

        zonal, meridional = split(0)
        temp, tracer = split(1)
        layer = [jnp.exp(jnp.where(small, got[u, 2 * i, :, lane(2)], got[u, 2 * i + 1, :, lane(2)])) for i in range(4)]
        lower = running(layer)
        upper = [x - y for x, y in zip(lower, layer)]
        bottom = lower[3][7:8]
        fields = (zonal, meridional, temp, tracer)
        before = []
        for f in fields:
            weighted = [x * y for x, y in zip(f, layer)]
            before.append([x - y for x, y in zip(running(weighted), weighted)])
        target = [bottom * bound[8 * i : 8 * i + 8, :] for i in range(4)]
        integral = [[] for _ in fields]
        ends = [lower[m][7:8] for m in range(3)]
        mids = [jnp.broadcast_to(lower[m][3:4], (8, 128)) for m in range(4)]
        for i in range(4):
            goal = target[i]
            past = [goal > e for e in ends]

            def pick(q):
                return jnp.where(past[2], q[3], jnp.where(past[1], q[2], jnp.where(past[0], q[1], q[0])))

            pos = jnp.where(pick(mids) < goal, 4, 0)
            pos = pos + jnp.where(pick([gather(x, pos + 1) for x in lower]) < goal, 2, 0)
            pos = pos + jnp.where(pick([gather(x, pos) for x in lower]) < goal, 1, 0)

            def here(q):
                return pick([gather(x, pos) for x in q])

            depth = goal - here(upper)
            for n, f in enumerate(fields):
                integral[n].append(here(before[n]) + depth * here(f))
        new_thick = [bottom * share[8 * i : 8 * i + 8, :] for i in range(4)]
        inverse = [1.0 / x for x in new_thick]
        remapped = [[(x - y) * z for x, y, z in zip(g, previous(g), inverse)] for g in integral]
        rise = [
            r * jnp.log((TOP_PRESSURE + x) / (TOP_PRESSURE + y))
            for r, x, y in zip(remapped[2], target, previous(target))
        ]
        geo = [None] * 4
        ground = surf[:, pl.ds(pl.multiple_of(t * 128, 128), 128)]
        carry = jnp.sum(jnp.where(sub == row, ground, 0.0), axis=0, keepdims=True)
        for i in (3, 2, 1, 0):
            x = rise[i]
            for d in (1, 2, 4):
                x = x + jnp.where(sub < 8 - d, pltpu.roll(x, 8 - d, 0), 0.0)
            geo[i] = x + carry
            carry = geo[i][0:1]
        pairs = ((remapped[0], remapped[1]), (remapped[2], remapped[3]), (geo, new_thick))
        for n, (one, two) in enumerate(pairs):
            for i in range(4):
                ret[u, 2 * i, :, lane(n)] = jnp.where(small, one[i], flip(two[i]))
                ret[u, 2 * i + 1, :, lane(n)] = jnp.where(small, flip(one[i]), two[i])
        lax.fori_loop(0, PEERS - 1, lambda k, z: (ret_copy(u, row, t, k).start(), z)[1], 0)
        back[t, row] = ret[u, lev]

    lax.fori_loop(5, 7, lambda m, z: (substep(1, 2 * m, 2 * m + 1), z)[1], 0)

    def front(h, depth):
        receive(0, h)
        receive(1, h)
        for n in range(1, min(depth, 3) + 1):
            substep(n, 8 + 2 * n - h, 15 - 2 * n + h)
        if depth == 4:
            release(8 - h, h - 1)

    def fronts(first, depth):
        def body(m, carry):
            h = first + 2 * m
            if relayed:
                pass_on(h + 1)
            front(h, depth)
            front(h + 1, depth)
            return carry

        return body

    lax.fori_loop(0, 1, fronts(1, 2), 0)
    lax.fori_loop(0, 1, fronts(3, 3), 0)
    lax.fori_loop(0, 2, fronts(5, 4), 0)

    def unit(n, carry):
        q = n // 2
        remap(jnp.where(n == 8, 8, jnp.where(n == 2 * q, 3 - q, 4 + q)))
        return carry

    lax.fori_loop(0, 9, unit, 0)

    def arrived(n, carry):
        u, k = n // (PEERS - 1), lax.rem(n, PEERS - 1)
        ret_copy(u, 0, 0, k).wait()
        return carry

    lax.fori_loop(0, 9 * (PEERS - 1), arrived, 0)

    def deliver(t, carry):
        for n in range(3):
            xs = [back[t, r, :, lane(n)] for r in range(ROWS)]
            for i, x in enumerate(transposed(xs)):
                result[64 * n + 8 * i : 64 * n + 8 * i + 8, pl.ds(pl.multiple_of(t * 128, 128), 128)] = x
        return carry

    lax.fori_loop(0, TILES, deliver, 0)

    outs = [
        pltpu.make_async_copy(result.at[pl.ds(at, size)], ref, out_sem.at[n])
        for n, (ref, at, size) in enumerate(((out_ref, 0, 128), (out_geo_ref, 128, 32), (out_thick_ref, 160, 32)))
    ]
    for copy in outs:
        copy.start()

    def sent(n, carry):
        u, k = n // (PEERS - 1), lax.rem(n, PEERS - 1)
        remote(fwd.at[0, 0], got.at[0, lev], fwd_send.at[u, k], fwd_recv.at[u, k], (lat, peer(k))).wait_send()
        return carry

    lax.fori_loop(0, 9 * (PEERS - 1), sent, 0)
    for h in range(1, ROWS + 1):
        pl.when(has_south)(lambda h=h: to_south(h).wait_send())
        pl.when(has_north)(lambda h=h: to_north(h).wait_send())
    if relayed:
        for h in range(2, ROWS + 1, 2):
            pl.when(relays_south)(lambda h=h: forward_south(h).wait_send())
            pl.when(relays_north)(lambda h=h: forward_north(h).wait_send())
    for copy in outs:
        copy.wait()


def shards(lat_size, velocity, potential_temp, tracer, thickness, surface_height, level_fractions):
    hbm = pl.BlockSpec(memory_space=pltpu.HBM)
    f32 = jnp.float32
    remapped, new_thickness, geopotential = pl.pallas_call(
        functools.partial(kernel, lat_size),
        out_shape=(
            jax.ShapeDtypeStruct((128, LON), f32),
            jax.ShapeDtypeStruct((32, LON), f32),
            jax.ShapeDtypeStruct((32, LON), f32),
        ),
        in_specs=[hbm] * 6,
        out_specs=(hbm,) * 3,
        scratch_shapes=[
            pltpu.SMEM((32,), f32),
            pltpu.VMEM((160, LON), f32),
            pltpu.VMEM((3 * ROWS, 8, ROW), f32),
            *[pltpu.VMEM((3 * ROWS, 8, LON), f32)] * 10,
            pltpu.VMEM((3 * ROWS, 8, 128), f32),
            pltpu.VMEM((32, 128), f32),
            pltpu.VMEM((32, 128), f32),
            pltpu.VMEM((ROWS, LON), f32),
            pltpu.VMEM((ROWS // 2, 8, ROW), f32),
            pltpu.VMEM((ROWS, TILES, 8, PIECE), f32),
            pltpu.VMEM((TILES, PEERS, 8, PIECE), f32),
            pltpu.VMEM((TILES, PEERS, 8, PIECE), f32),
            pltpu.VMEM((TILES, ROWS, 8, PIECE), f32),
            pltpu.VMEM((192, LON), f32),
            pltpu.SemaphoreType.DMA((6,)),
            pltpu.SemaphoreType.DMA((2, ROWS)),
            pltpu.SemaphoreType.DMA((2, ROWS)),
            pltpu.SemaphoreType.DMA((ROWS // 2,)),
            pltpu.SemaphoreType.DMA((ROWS // 2,)),
            pltpu.SemaphoreType.DMA((9, PEERS - 1)),
            pltpu.SemaphoreType.DMA((9, PEERS - 1)),
            pltpu.SemaphoreType.DMA((9, PEERS - 1)),
            pltpu.SemaphoreType.DMA((9, PEERS - 1)),
            pltpu.SemaphoreType.DMA((3,)),
        ],
        compiler_params=pltpu.CompilerParams(
            collective_id=0, has_side_effects=True, vmem_limit_bytes=63 * 2**20
        ),
        cost_estimate=pl.CostEstimate(flops=10**8, bytes_accessed=2 * 10**6, transcendentals=10**6),
    )(
        velocity.reshape(64, LON),
        potential_temp.reshape(32, LON),
        tracer.reshape(32, LON),
        thickness.reshape(32, LON),
        surface_height,
        level_fractions,
    )
    return (
        remapped.reshape(4, 4, ROWS, LON),
        new_thickness.reshape(4, ROWS, LON),
        geopotential.reshape(4, ROWS, LON),
    )


def solution(mesh):
    return jax.shard_map(
        functools.partial(shards, mesh.shape["lat"]),
        mesh=mesh,
        in_specs=(
            P(None, "lev", "lat", None),
            P("lev", "lat", None),
            P("lev", "lat", None),
            P("lev", "lat", None),
            P("lat", None),
            P(),
        ),
        out_specs=(P(None, "lev", "lat", None), P("lev", "lat", None), P("lev", "lat", None)),
        check_vma=False,
    )
```

time: 63.4 us -> 52.8 us (0.83)
  the two profiles are of different devices: /device:TPU:8 before, /device:TPU:192 now
where the time goes in v2:
time: 52.8 us; the launch traced here: 52.7 us
  Pallas kernels  48.4 us (92%)
  local copies, waits for them, and re-layouts  3.58 us (7%)
  between operations  0.65 us (1%)
    pallas_call x1, Pallas kernels, shards(): pl.pallas_call(functools.partial(kernel, lat_size), out_shape=(jax.ShapeD...  48.4 us
    unnamed x7, local copies, waits for them, and re-layouts  3.58 us

profile of v2, /device:TPU:192, one launch (start us, length us, event | category | flops | bytes accessed | tf_op | source)
XLA Modules:
  0.0 52.7 jit_solution(5598035535793964272)
XLA Ops:
  0.6 48.4 %shard_map.85 = (f32[128,1152]{1,0:T(8,128)}, f32[32,1152]{1,0:T(8,128)}, f32[32,1152]{1,0:T(8,128)}) custom-call(f32[64,1152]{1,0:T(8,128)} %bitcast.10, f32[32,1152]{1,0:T(8,128)} %bitcast.11, f32[32,1152]{1,0:T(8,128)} %bitcast.12, f32[32,1152]{1,0:T(8,128)} %bitcast.13, f32[8,1152]{1,0:T(8,128)} %surf_ref.1, f32[32]{0:T(128)} %frac_ref.1), custom_call_target="tpu_custom_call" | custom-call | flops 100000000 | bytes 2000000 | tf_op jit(solution)/shard_map/pallas_call | solution.py:508
  49.1 0.0 copy-start.1
  49.1 2.0 %copy.12 = f32[4,4,8,1152]{3,2,1,0:T(8,128)} copy(f32[4,4,8,1152]{3,2,1,0:T(8,128)} %bitcast.7) | data formatting | bytes 1179648
  51.0 0.0 copy-done.1
  51.0 0.0 copy-start
  51.0 0.7 %copy.13 = f32[4,8,1152]{2,1,0:T(8,128)} copy(f32[4,8,1152]{2,1,0:T(8,128)S(1)} %bitcast.9) | data formatting | bytes 294912
  51.7 0.3 copy-done
  52.0 0.7 %copy.14 = f32[4,8,1152]{2,1,0:T(8,128)} copy(f32[4,8,1152]{2,1,0:T(8,128)S(1)} %bitcast.8) | data formatting | bytes 294912
Async XLA Ops:
  49.1 2.0 %copy-start.1 = (f32[32,1152]{1,0:T(8,128)S(1)}, f32[32,1152]{1,0:T(8,128)}, u32[]{:S(2)}) copy-start(f32[32,1152]{1,0:T(8,128)} %get-tuple-element.7) | copy-start | bytes 442372
  51.0 1.0 %copy-start = (f32[32,1152]{1,0:T(8,128)S(1)}, f32[32,1152]{1,0:T(8,128)}, u32[]{:S(2)}) copy-start(f32[32,1152]{1,0:T(8,128)} %get-tuple-element.8) | copy-start | bytes 442372

commit v3 on v2

--- a/solution.py
+++ b/solution.py
@@ -20,17 +20,19 @@
 TILES = 9
 ROW = 2 * LON + 640
 PIECE = 384
+PAIR = 640
 PEERS = 8
 RING = 8
+RELAYED = (3, 5, 7)
 
 
 def kernel(
     lat_size,
     vel_ref, temp_ref, tracer_ref, thick_ref, surf_ref, frac_ref,
     out_ref, out_thick_ref, out_geo_ref,
-    frac, band, rows, s_0, uv_1, pq_1, s_1, uv_2, pq_2, s_2, uv_3, pq_3, s_3, turn, bound, share, surf,
-    relay, fwd, got, ret, back, result,
-    local_sem, halo_send, halo_recv, relay_send, relay_recv, fwd_send, fwd_recv, ret_send, ret_recv, out_sem,
+    frac, band, rows, s_0, uv_1, pq_1, s_1, uv_2, pq_2, s_2, uv_3, pq_3, s_3, turn, bound, share, splat, surf,
+    relay, fwd, extra, s_4, got, ret, bottoms, back,
+    local_sem, halo_send, halo_recv, relay_send, relay_recv, fwd_send, fwd_recv, ret_send, ret_recv,
 ):
     lat, lev = lax.axis_index("lat"), lax.axis_index("lev")
     relayed = lat_size % RING == 0 and lat_size > RING
@@ -154,12 +156,12 @@
         )
 
     def to_relay(way, h):
-        n = h // 2 - 1
+        n = RELAYED.index(h)
         src = rows.at[2 * ROWS - h] if way == 0 else rows.at[ROWS - 1 + h]
         return remote(src, relay.at[n], halo_send.at[way, h - 1], relay_recv.at[n], (beside, lev))
 
     for h in range(1, ROWS + 1):
-        if relayed and h % 2 == 0:
+        if relayed and h in RELAYED:
             pl.when(has_south & before_step)(lambda h=h: to_relay(0, h).start())
             pl.when(has_south & jnp.logical_not(before_step))(lambda h=h: to_south(h).start())
             pl.when(has_north & after_step)(lambda h=h: to_relay(1, h).start())
@@ -169,10 +171,10 @@
             pl.when(has_north)(lambda h=h: to_north(h).start())
 
     def forward_south(h):
-        return to_south(h, relay.at[h // 2 - 1], band_at(RING), relay_send.at[h // 2 - 1])
+        return to_south(h, relay.at[RELAYED.index(h)], band_at(RING), relay_send.at[RELAYED.index(h)])
 
     def forward_north(h):
-        return to_north(h, relay.at[h // 2 - 1], band_at(-RING), relay_send.at[h // 2 - 1])
+        return to_north(h, relay.at[RELAYED.index(h)], band_at(-RING), relay_send.at[RELAYED.index(h)])
 
     def pass_on(h):
         @pl.when(relays_south)
@@ -191,9 +193,11 @@
     for k in range(4 * PEERS):
         total = total + frac[k]
         share[k, :] = jnp.full((128,), frac[k], jnp.float32)
+        splat[k] = jnp.full((8, 128), frac[k], jnp.float32)
         bound[k, :] = jnp.full((128,), total, jnp.float32)
     share[...] = share[...] / total
     bound[...] = bound[...] / total
+    bottoms[...] = jnp.zeros((8, 128), jnp.float32)
     row_of = lax.broadcasted_iota(jnp.int32, (3 * ROWS, 8, 128), 0) + (lat - 1) * ROWS
     angle = -0.5 * math.pi + (row_of.astype(jnp.float32) + 0.5) * (math.pi / (lat_size * ROWS))
     sign = jnp.where(lax.broadcasted_iota(jnp.int32, (3 * ROWS, 8, 128), 1) < 4, ROTATION_RATE, -ROTATION_RATE)
@@ -298,39 +302,54 @@
             if t < 4:
                 s_0[j, :, lane(t + 5)] = jnp.where(small, y, x)
 
-    def fwd_copy(r, step):
-        t = lax.rem(peer(step) - r + PEERS, PEERS)
-        return remote(
-            fwd.at[r, t], got.at[r, lev], fwd_send.at[r, step], fwd_recv.at[r, step], (lat, peer(step))
-        )
-
-    def extra_copy(r):
-        step = lax.rem(r - lev - 1 + 2 * PEERS, PEERS)
-        return remote(fwd.at[r, 8], got.at[8, lev], fwd_send.at[8, step], fwd_recv.at[8, step], (lat, r))
-
-    def release(*rs):
-        def into(r):
+    def fwd_copy(q, step):
+        to = peer(step)
+        return remote(fwd.at[q, to], got.at[q, lev], fwd_send.at[q, step], fwd_recv.at[q, step], (lat, to))
+
+    def extra_copy(q, side, to, step):
+        dst = got.at[4, lev, :, pl.ds(0, PIECE)]
+        return remote(extra.at[q, side], dst, fwd_send.at[4, step], fwd_recv.at[4, step], (lat, to))
+
+    def release(q):
+        pair = (3 - q, 4 + q)
+
+        def into(side, r):
+            at = side * PIECE
+
             def emit(t, new_uv, new_pq, new_s):
-                fwd[r, t, :, lane(0)] = new_uv
-                fwd[r, t, :, lane(1)] = new_pq
-                fwd[r, t, :, lane(2)] = new_s
+                if t < 8:
+                    to = lax.rem(r + t, PEERS)
+                    fwd[q, to, :, at : at + 128] = new_uv
+                    fwd[q, to, :, at + 128 : at + 256] = new_pq
+                    s_4[side, to] = new_s
+                else:
+                    extra[q, side, :, lane(0)] = new_uv
+                    extra[q, side, :, lane(1)] = new_pq
+                    extra[q, side, :, lane(2)] = new_s
 
             return emit
 
-        advance(states[3], [ROWS + r for r in rs], [into(r) for r in rs])
-        for r in rs:
-            lax.fori_loop(0, PEERS - 1, lambda k, z, r=r: (fwd_copy(r, k).start(), z)[1], 0)
-            pl.when(r != lev)(lambda r=r: extra_copy(r).start())
-            got[r, lev] = fwd[r, lax.rem(lev - r + PEERS, PEERS)]
+        advance(states[3], [ROWS + r for r in pair], [into(side, r) for side, r in enumerate(pair)])
+        for to in range(PEERS):
+            fwd[q, to, :, lane(2)] = jnp.where(small, s_4[0, to], s_4[1, to])
+        lax.fori_loop(0, PEERS - 1, lambda k, z: (fwd_copy(q, k).start(), z)[1], 0)
+        got[q, lev] = fwd[q, lev]
+        for side, r in enumerate(pair):
+            step = lax.rem(r - lev - 1 + 2 * PEERS, PEERS)
+            pl.when(r != lev)(lambda side=side, r=r, step=step: extra_copy(q, side, r, step).start())
 
             @pl.when(r == lev)
-            def _(r=r):
-                got[8, lev] = fwd[r, 8]
-
-    def ret_copy(u, row, t, step):
-        return remote(
-            ret.at[u, peer(step)], back.at[t, row], ret_send.at[u, step], ret_recv.at[u, step], (lat, peer(step))
-        )
+            def _(side=side):
+                got[4, lev, :, 0:PIECE] = extra[q, side]
+
+    def ret_copy(q, step):
+        to = peer(step)
+        return remote(ret.at[q, to], back.at[q, lev], ret_send.at[q, step], ret_recv.at[q, step], (lat, to))
+
+    def last_copy(step):
+        to, lanes = peer(step), pl.ds(0, 512)
+        dst = back.at[4, lev, :, lanes]
+        return remote(ret.at[4, to, :, lanes], dst, ret_send.at[4, step], ret_recv.at[4, step], (lat, to))
 
     def running(values):
         out, carry = [], None
@@ -353,30 +372,26 @@
     def gather(x, index):
         return jnp.take_along_axis(x, index, axis=0, mode="promise_in_bounds")
 
-    def remap(u):
-        row = jnp.where(u < 8, u, lev)
-        t = jnp.where(u < 8, lax.rem(lev - u + 2 * PEERS, PEERS), 8)
-        lax.fori_loop(
-            0,
-            PEERS - 1,
-            lambda k, z: (
-                remote(
-                    fwd.at[0, 0], got.at[u, lev], fwd_send.at[u, k], fwd_recv.at[u, k], (lat, peer(k))
-                ).wait_recv(),
-                z,
-            )[1],
-            0,
-        )
+    def remap(q, side):
+        first = side == 0
+        row = jnp.where(q == 4, lev, jnp.where(first, 3 - q, 4 + q))
+        t = jnp.where(q == 4, 8, lax.rem(lev - row + 2 * PEERS, PEERS))
+        at = side * PIECE
 
         def split(n):
-            xs = [got[u, p, :, lane(n)] for p in range(PEERS)]
-            first = [jnp.where(small, xs[2 * i], flip(xs[2 * i + 1])) for i in range(4)]
-            second = [jnp.where(small, flip(xs[2 * i]), xs[2 * i + 1]) for i in range(4)]
-            return first, second
+            xs = [got[q, p, :, pl.ds(pl.multiple_of(at + 128 * n, 128), 128)] for p in range(PEERS)]
+            one = [jnp.where(small, xs[2 * i], flip(xs[2 * i + 1])) for i in range(4)]
+            two = [jnp.where(small, flip(xs[2 * i]), xs[2 * i + 1]) for i in range(4)]
+            return one, two
 
         zonal, meridional = split(0)
         temp, tracer = split(1)
-        layer = [jnp.exp(jnp.where(small, got[u, 2 * i, :, lane(2)], got[u, 2 * i + 1, :, lane(2)])) for i in range(4)]
+        xs = [got[q, p, :, lane(2)] for p in range(PEERS)]
+        layer = []
+        for i in range(4):
+            one = jnp.where(small, xs[2 * i], flip(xs[2 * i + 1]))
+            two = jnp.where(small, flip(xs[2 * i]), xs[2 * i + 1])
+            layer.append(jnp.exp(jnp.where(first, one, two)))
         lower = running(layer)
         upper = [x - y for x, y in zip(lower, layer)]
         bottom = lower[3][7:8]
@@ -393,15 +408,15 @@
             goal = target[i]
             past = [goal > e for e in ends]
 
-            def pick(q):
-                return jnp.where(past[2], q[3], jnp.where(past[1], q[2], jnp.where(past[0], q[1], q[0])))
+            def pick(x):
+                return jnp.where(past[2], x[3], jnp.where(past[1], x[2], jnp.where(past[0], x[1], x[0])))
 
             pos = jnp.where(pick(mids) < goal, 4, 0)
             pos = pos + jnp.where(pick([gather(x, pos + 1) for x in lower]) < goal, 2, 0)
             pos = pos + jnp.where(pick([gather(x, pos) for x in lower]) < goal, 1, 0)
 
-            def here(q):
-                return pick([gather(x, pos) for x in q])
+            def here(xs):
+                return pick([gather(x, pos) for x in xs])
 
             depth = goal - here(upper)
             for n, f in enumerate(fields):
@@ -422,13 +437,25 @@
                 x = x + jnp.where(sub < 8 - d, pltpu.roll(x, 8 - d, 0), 0.0)
             geo[i] = x + carry
             carry = geo[i][0:1]
-        pairs = ((remapped[0], remapped[1]), (remapped[2], remapped[3]), (geo, new_thick))
-        for n, (one, two) in enumerate(pairs):
+        for n, (one, two) in enumerate(((remapped[0], remapped[1]), (remapped[2], remapped[3]))):
+            lanes = pl.ds(pl.multiple_of(at + 128 * n, 128), 128)
             for i in range(4):
-                ret[u, 2 * i, :, lane(n)] = jnp.where(small, one[i], flip(two[i]))
-                ret[u, 2 * i + 1, :, lane(n)] = jnp.where(small, flip(one[i]), two[i])
-        lax.fori_loop(0, PEERS - 1, lambda k, z: (ret_copy(u, row, t, k).start(), z)[1], 0)
-        back[t, row] = ret[u, lev]
+                ret[q, 2 * i, :, lanes] = jnp.where(small, one[i], flip(two[i]))
+                ret[q, 2 * i + 1, :, lanes] = jnp.where(small, flip(one[i]), two[i])
+        mine = jnp.where(first, sub, 7 - sub) < 4
+        floor = jnp.broadcast_to(bottom, (8, 128))
+        for i in range(4):
+            flipped = flip(geo[i])
+            for p, x in ((2 * i, jnp.where(first, geo[i], flipped)), (2 * i + 1, jnp.where(first, flipped, geo[i]))):
+                other = jnp.where(first, floor, ret[q, p, :, lane(2)])
+                ret[q, p, :, lane(2)] = jnp.where(mine, x, other)
+        bottoms[...] = jnp.where((sub == row) & (q < 4), floor, bottoms[...])
+
+    def process(q):
+        lax.fori_loop(0, PEERS - 1, lambda k, z: (fwd_copy(q, k).wait_recv(), z)[1], 0)
+        lax.fori_loop(0, 2, lambda side, z: (remap(q, side), z)[1], 0)
+        lax.fori_loop(0, PEERS - 1, lambda k, z: (ret_copy(q, k).start(), z)[1], 0)
+        back[q, lev] = ret[q, lev]
 
     lax.fori_loop(5, 7, lambda m, z: (substep(1, 2 * m, 2 * m + 1), z)[1], 0)
 
@@ -438,68 +465,83 @@
         for n in range(1, min(depth, 3) + 1):
             substep(n, 8 + 2 * n - h, 15 - 2 * n + h)
         if depth == 4:
-            release(8 - h, h - 1)
-
-    def fronts(first, depth):
-        def body(m, carry):
-            h = first + 2 * m
-            if relayed:
-                pass_on(h + 1)
-            front(h, depth)
-            front(h + 1, depth)
-            return carry
-
-        return body
-
-    lax.fori_loop(0, 1, fronts(1, 2), 0)
-    lax.fori_loop(0, 1, fronts(3, 3), 0)
-    lax.fori_loop(0, 2, fronts(5, 4), 0)
-
-    def unit(n, carry):
-        q = n // 2
-        remap(jnp.where(n == 8, 8, jnp.where(n == 2 * q, 3 - q, 4 + q)))
+            release(h - 5)
+
+    def passing(h):
+        if relayed:
+            pass_on(h)
+
+    def late(m, carry):
+        front(5 + 2 * m, 4)
+        pl.when(m == 1)(lambda: process(0))
+        front(6 + 2 * m, 4)
+        pl.when(m == 1)(lambda: process(1))
         return carry
 
-    lax.fori_loop(0, 9, unit, 0)
-
-    def arrived(n, carry):
-        u, k = n // (PEERS - 1), lax.rem(n, PEERS - 1)
-        ret_copy(u, 0, 0, k).wait()
+    passing(3)
+    front(1, 2)
+    passing(5)
+    front(2, 2)
+    passing(7)
+    front(3, 3)
+    front(4, 3)
+    lax.fori_loop(0, 2, late, 0)
+    lax.fori_loop(2, 4, lambda q, z: (process(q), z)[1], 0)
+    lax.fori_loop(0, PEERS - 1, lambda k, z: (extra_copy(0, 0, 0, k).wait_recv(), z)[1], 0)
+    remap(4, 0)
+    for p in range(PEERS):
+        ret[4, p, :, lane(3)] = bottoms[...]
+    lax.fori_loop(0, PEERS - 1, lambda k, z: (last_copy(k).start(), z)[1], 0)
+    back[4, lev, :, 0:512] = ret[4, lev, :, 0:512]
+
+    for q in range(4):
+        lax.fori_loop(0, PEERS - 1, lambda k, z, q=q: (ret_copy(q, k).wait(), z)[1], 0)
+    lax.fori_loop(0, PEERS - 1, lambda k, z: (last_copy(k).wait(), z)[1], 0)
+
+    def put(lanes, uv, pq, geo, bottom):
+        for at, xs in ((0, uv), (64, pq)):
+            for i, x in enumerate(transposed(xs)):
+                out_ref[at + 8 * i : at + 8 * i + 8, lanes] = x
+        for i, x in enumerate(transposed(geo)[:4]):
+            out_geo_ref[8 * i : 8 * i + 8, lanes] = x
+            out_thick_ref[8 * i : 8 * i + 8, lanes] = bottom * (splat[4 * lev + i] / total)
+
+    def deliver(t, carry):
+        uv, pq, geo = [], [], []
+        bottom = jnp.zeros((8, 128), jnp.float32)
+        for r in range(ROWS):
+            owner, q, side = lax.rem(r + t, PEERS), max(3 - r, r - 4), r // 4
+            uv.append(back[q, owner, :, side * PIECE : side * PIECE + 128])
+            pq.append(back[q, owner, :, side * PIECE + 128 : side * PIECE + 256])
+            x = back[q, owner, :, lane(2)]
+            geo.append(flip(x) if side else x)
+            bottom = jnp.where(sub == r, back[4, owner, :, lane(3)], bottom)
+        put(pl.ds(pl.multiple_of(t * 128, 128), 128), uv, pq, geo, bottom)
         return carry
 
-    lax.fori_loop(0, 9 * (PEERS - 1), arrived, 0)
-
-    def deliver(t, carry):
-        for n in range(3):
-            xs = [back[t, r, :, lane(n)] for r in range(ROWS)]
-            for i, x in enumerate(transposed(xs)):
-                result[64 * n + 8 * i : 64 * n + 8 * i + 8, pl.ds(pl.multiple_of(t * 128, 128), 128)] = x
-        return carry
-
-    lax.fori_loop(0, TILES, deliver, 0)
-
-    outs = [
-        pltpu.make_async_copy(result.at[pl.ds(at, size)], ref, out_sem.at[n])
-        for n, (ref, at, size) in enumerate(((out_ref, 0, 128), (out_geo_ref, 128, 32), (out_thick_ref, 160, 32)))
-    ]
-    for copy in outs:
-        copy.start()
-
-    def sent(n, carry):
-        u, k = n // (PEERS - 1), lax.rem(n, PEERS - 1)
-        remote(fwd.at[0, 0], got.at[0, lev], fwd_send.at[u, k], fwd_recv.at[u, k], (lat, peer(k))).wait_send()
-        return carry
-
-    lax.fori_loop(0, 9 * (PEERS - 1), sent, 0)
+    lax.fori_loop(0, TILES - 1, deliver, 0)
+    geo = [back[4, r, :, lane(2)] for r in range(ROWS)]
+    bottom = jnp.zeros((8, 128), jnp.float32)
+    for r in range(ROWS):
+        bottom = jnp.where(sub == r, geo[r] if r >= 4 else flip(geo[r]), bottom)
+    put(
+        lane(8),
+        [back[4, r, :, lane(0)] for r in range(ROWS)],
+        [back[4, r, :, lane(1)] for r in range(ROWS)],
+        geo,
+        bottom,
+    )
+
+    for q in range(4):
+        lax.fori_loop(0, PEERS - 1, lambda k, z, q=q: (fwd_copy(q, k).wait_send(), z)[1], 0)
+    lax.fori_loop(0, PEERS - 1, lambda k, z: (extra_copy(0, 0, 0, k).wait_send(), z)[1], 0)
     for h in range(1, ROWS + 1):
         pl.when(has_south)(lambda h=h: to_south(h).wait_send())
         pl.when(has_north)(lambda h=h: to_north(h).wait_send())
     if relayed:
-        for h in range(2, ROWS + 1, 2):
+        for h in RELAYED:
             pl.when(relays_south)(lambda h=h: forward_south(h).wait_send())
             pl.when(relays_north)(lambda h=h: forward_north(h).wait_send())
-    for copy in outs:
-        copy.wait()
 
 
 def shards(lat_size, velocity, potential_temp, tracer, thickness, surface_height, level_fractions):
@@ -513,7 +555,7 @@
             jax.ShapeDtypeStruct((32, LON), f32),
         ),
         in_specs=[hbm] * 6,
-        out_specs=(hbm,) * 3,
+        out_specs=(pl.BlockSpec(memory_space=pltpu.VMEM),) * 3,
         scratch_shapes=[
             pltpu.SMEM((32,), f32),
             pltpu.VMEM((160, LON), f32),
@@ -522,26 +564,28 @@
             pltpu.VMEM((3 * ROWS, 8, 128), f32),
             pltpu.VMEM((32, 128), f32),
             pltpu.VMEM((32, 128), f32),
+            pltpu.VMEM((32, 8, 128), f32),
             pltpu.VMEM((ROWS, LON), f32),
-            pltpu.VMEM((ROWS // 2, 8, ROW), f32),
-            pltpu.VMEM((ROWS, TILES, 8, PIECE), f32),
-            pltpu.VMEM((TILES, PEERS, 8, PIECE), f32),
-            pltpu.VMEM((TILES, PEERS, 8, PIECE), f32),
-            pltpu.VMEM((TILES, ROWS, 8, PIECE), f32),
-            pltpu.VMEM((192, LON), f32),
+            pltpu.VMEM((len(RELAYED), 8, ROW), f32),
+            pltpu.VMEM((4, PEERS, 8, PAIR), f32),
+            pltpu.VMEM((4, 2, 8, PIECE), f32),
+            pltpu.VMEM((2, PEERS, 8, 128), f32),
+            pltpu.VMEM((5, PEERS, 8, PAIR), f32),
+            pltpu.VMEM((5, PEERS, 8, PAIR), f32),
+            pltpu.VMEM((8, 128), f32),
+            pltpu.VMEM((5, PEERS, 8, PAIR), f32),
             pltpu.SemaphoreType.DMA((6,)),
             pltpu.SemaphoreType.DMA((2, ROWS)),
             pltpu.SemaphoreType.DMA((2, ROWS)),
-            pltpu.SemaphoreType.DMA((ROWS // 2,)),
-            pltpu.SemaphoreType.DMA((ROWS // 2,)),
-            pltpu.SemaphoreType.DMA((9, PEERS - 1)),
-            pltpu.SemaphoreType.DMA((9, PEERS - 1)),
-            pltpu.SemaphoreType.DMA((9, PEERS - 1)),
-            pltpu.SemaphoreType.DMA((9, PEERS - 1)),
-            pltpu.SemaphoreType.DMA((3,)),
+            pltpu.SemaphoreType.DMA((len(RELAYED),)),
+            pltpu.SemaphoreType.DMA((len(RELAYED),)),
+            pltpu.SemaphoreType.DMA((5, PEERS - 1)),
+            pltpu.SemaphoreType.DMA((5, PEERS - 1)),
+            pltpu.SemaphoreType.DMA((5, PEERS - 1)),
+            pltpu.SemaphoreType.DMA((5, PEERS - 1)),
         ],
         compiler_params=pltpu.CompilerParams(
-            collective_id=0, has_side_effects=True, vmem_limit_bytes=63 * 2**20
+            collective_id=0, has_side_effects=True, vmem_limit_bytes=64 * 2**20 - 6 * 32 * LON * 4 - 4096
         ),
         cost_estimate=pl.CostEstimate(flops=10**8, bytes_accessed=2 * 10**6, transcendentals=10**6),
     )(

time: 52.8 us -> 46.5 us (0.88)
  the two profiles are of different devices: /device:TPU:192 before, /device:TPU:128 now
where the time goes in v3:
time: 46.5 us; the launch traced here: 46.3 us
  Pallas kernels  42.1 us (91%)
  local copies, waits for them, and re-layouts  3.58 us (8%)
  between operations  0.65 us (1%)
    pallas_call x1, Pallas kernels, shards(): pl.pallas_call(functools.partial(kernel, lat_size), out_shape=(jax.ShapeD...  42.1 us
    unnamed x7, local copies, waits for them, and re-layouts  3.58 us

profile of v3, /device:TPU:128, one launch (start us, length us, event | category | flops | bytes accessed | tf_op | source)
XLA Modules:
  0.0 46.3 jit_solution(4484487410304613773)
XLA Ops:
  0.6 42.1 %shard_map.85 = (f32[128,1152]{1,0:T(8,128)}, f32[32,1152]{1,0:T(8,128)}, f32[32,1152]{1,0:T(8,128)}) custom-call(f32[64,1152]{1,0:T(8,128)} %bitcast.10, f32[32,1152]{1,0:T(8,128)} %bitcast.11, f32[32,1152]{1,0:T(8,128)} %bitcast.12, f32[32,1152]{1,0:T(8,128)} %bitcast.13, f32[8,1152]{1,0:T(8,128)} %surf_ref.1, f32[32]{0:T(128)} %frac_ref.1), custom_call_target="tpu_custom_call" | custom-call | flops 100000000 | bytes 2000000 | tf_op jit(solution)/shard_map/pallas_call | solution.py:550
  42.7 0.0 copy-start.1
  42.7 2.0 %copy.12 = f32[4,4,8,1152]{3,2,1,0:T(8,128)} copy(f32[4,4,8,1152]{3,2,1,0:T(8,128)} %bitcast.7) | data formatting | bytes 1179648
  44.7 0.0 copy-done.1
  44.7 0.0 copy-start
  44.7 0.7 %copy.13 = f32[4,8,1152]{2,1,0:T(8,128)} copy(f32[4,8,1152]{2,1,0:T(8,128)S(1)} %bitcast.9) | data formatting | bytes 294912
  45.4 0.3 copy-done
  45.7 0.7 %copy.14 = f32[4,8,1152]{2,1,0:T(8,128)} copy(f32[4,8,1152]{2,1,0:T(8,128)S(1)} %bitcast.8) | data formatting | bytes 294912
Async XLA Ops:
  42.7 2.0 %copy-start.1 = (f32[32,1152]{1,0:T(8,128)S(1)}, f32[32,1152]{1,0:T(8,128)}, u32[]{:S(2)}) copy-start(f32[32,1152]{1,0:T(8,128)} %get-tuple-element.7) | copy-start | bytes 442372
  44.7 1.0 %copy-start = (f32[32,1152]{1,0:T(8,128)S(1)}, f32[32,1152]{1,0:T(8,128)}, u32[]{:S(2)}) copy-start(f32[32,1152]{1,0:T(8,128)} %get-tuple-element.8) | copy-start | bytes 442372

commit v4 on v3

--- a/solution.py
+++ b/solution.py
@@ -544,16 +544,31 @@
             pl.when(relays_north)(lambda h=h: forward_north(h).wait_send())
 
 
+def publish(remapped, thick, geo, out_ref, out_thick_ref, out_geo_ref, held, sem):
+    pairs = [(remapped.at[pl.ds(32 * n, 32)], out_ref.at[pl.ds(32 * n, 32)]) for n in range(4)]
+    pairs += [(thick, out_thick_ref), (geo, out_geo_ref)]
+    reads = [pltpu.make_async_copy(src, held.at[n], sem.at[0, n]) for n, (src, _) in enumerate(pairs)]
+    writes = [pltpu.make_async_copy(held.at[n], dst, sem.at[1, n]) for n, (_, dst) in enumerate(pairs)]
+    for copy in reads:
+        copy.start()
+    for read, write in zip(reads, writes):
+        read.wait()
+        write.start()
+    for copy in writes:
+        copy.wait()
+
+
 def shards(lat_size, velocity, potential_temp, tracer, thickness, surface_height, level_fractions):
     hbm = pl.BlockSpec(memory_space=pltpu.HBM)
     f32 = jnp.float32
-    remapped, new_thickness, geopotential = pl.pallas_call(
+    out_shape = (
+        jax.ShapeDtypeStruct((128, LON), f32),
+        jax.ShapeDtypeStruct((32, LON), f32),
+        jax.ShapeDtypeStruct((32, LON), f32),
+    )
+    results = pl.pallas_call(
         functools.partial(kernel, lat_size),
-        out_shape=(
-            jax.ShapeDtypeStruct((128, LON), f32),
-            jax.ShapeDtypeStruct((32, LON), f32),
-            jax.ShapeDtypeStruct((32, LON), f32),
-        ),
+        out_shape=out_shape,
         in_specs=[hbm] * 6,
         out_specs=(pl.BlockSpec(memory_space=pltpu.VMEM),) * 3,
         scratch_shapes=[
@@ -585,7 +600,7 @@
             pltpu.SemaphoreType.DMA((5, PEERS - 1)),
         ],
         compiler_params=pltpu.CompilerParams(
-            collective_id=0, has_side_effects=True, vmem_limit_bytes=64 * 2**20 - 6 * 32 * LON * 4 - 4096
+            collective_id=0, has_side_effects=True, vmem_limit_bytes=60 * 2**20
         ),
         cost_estimate=pl.CostEstimate(flops=10**8, bytes_accessed=2 * 10**6, transcendentals=10**6),
     )(
@@ -596,6 +611,15 @@
         surface_height,
         level_fractions,
     )
+    remapped, new_thickness, geopotential = pl.pallas_call(
+        publish,
+        out_shape=out_shape,
+        in_specs=[hbm] * 3,
+        out_specs=(hbm,) * 3,
+        scratch_shapes=[pltpu.VMEM((6, 32, LON), f32), pltpu.SemaphoreType.DMA((2, 6))],
+        compiler_params=pltpu.CompilerParams(vmem_limit_bytes=60 * 2**20),
+        cost_estimate=pl.CostEstimate(flops=0, bytes_accessed=2 * 10**6, transcendentals=0),
+    )(*results)
     return (
         remapped.reshape(4, 4, ROWS, LON),
         new_thickness.reshape(4, ROWS, LON),

time: 46.5 us -> 44.9 us (0.966)
  local copies, waits for them, and re-layouts: 3.58 us -> 0 us
  Pallas kernels: 42.1 us -> 44.1 us
    unnamed x7 -> x0, local copies, waits for them, and re-layouts: 3.58 us -> none
    pallas_call x1 -> x2, Pallas kernels: 42.1 us -> 44.1 us  [the longest x1 42.1 us: shards(): pl.pallas_call(functools.partial(kernel, lat_size), out_shape=out_shape,...]
where the time goes in v4:
time: 44.9 us; the launch traced here: 44.8 us
  Pallas kernels  44.1 us (98%)
  between operations  0.64 us (1%)
    pallas_call x1, Pallas kernels, shards(): pl.pallas_call(functools.partial(kernel, lat_size), out_shape=out_shape,...  42.1 us
    pallas_call x1, Pallas kernels, shards(): pl.pallas_call(publish, out_shape=out_shape, in_specs=[hbm] * 3, out_spec...  2.02 us

profile of v4, /device:TPU:128, one launch (start us, length us, event | category | flops | bytes accessed | tf_op | source)
XLA Modules:
  0.0 44.8 jit_solution(10274558384720849088)
XLA Ops:
  0.6 42.1 %shard_map.85 = (f32[128,1152]{1,0:T(8,128)}, f32[32,1152]{1,0:T(8,128)}, f32[32,1152]{1,0:T(8,128)}) custom-call(f32[64,1152]{1,0:T(8,128)} %bitcast.8, f32[32,1152]{1,0:T(8,128)} %bitcast.9, f32[32,1152]{1,0:T(8,128)} %bitcast.10, f32[32,1152]{1,0:T(8,128)} %bitcast.11, f32[8,1152]{1,0:T(8,128)} %surf_ref.1, f32[32]{0:T(128)} %frac_ref.1), custom_call_target="tpu_custom_call" | custom-call | flops 100000000 | bytes 2000000 | tf_op jit(solution)/shard_map/pallas_call | solution.py:569
  42.7 2.0 %shard_map.86 = (f32[128,1152]{1,0:T(8,128)}, f32[32,1152]{1,0:T(8,128)}, f32[32,1152]{1,0:T(8,128)}) custom-call(f32[128,1152]{1,0:T(8,128)} %get-tuple-element.9.remapped, f32[32,1152]{1,0:T(8,128)} %get-tuple-element.10.thick, f32[32,1152]{1,0:T(8,128)} %get-tuple-element.11.geo), custom_call_target="tpu_custom_call" | custom-call | bytes 2000000 | tf_op jit(solution)/shard_map/pallas_call | solution.py:614

commit v5 on v4

--- a/solution.py
+++ b/solution.py
@@ -26,13 +26,29 @@
 RELAYED = (3, 5, 7)
 
 
+def flip(x):
+    return pltpu.roll(x, 4, 0)
+
+
+def transposed(xs):
+    sub = lax.broadcasted_iota(jnp.int32, (8, 128), 0)
+    for d in (4, 2, 1):
+        ys = list(xs)
+        for i in range(8):
+            if not i & d:
+                ys[i] = jnp.where(sub & d == 0, xs[i], pltpu.roll(xs[i + d], d, 0))
+                ys[i + d] = jnp.where(sub & d == 0, pltpu.roll(xs[i], 8 - d, 0), xs[i + d])
+        xs = ys
+    return xs
+
+
 def kernel(
     lat_size,
     vel_ref, temp_ref, tracer_ref, thick_ref, surf_ref, frac_ref,
-    out_ref, out_thick_ref, out_geo_ref,
-    frac, band, rows, s_0, uv_1, pq_1, s_1, uv_2, pq_2, s_2, uv_3, pq_3, s_3, turn, bound, share, splat, surf,
-    relay, fwd, extra, s_4, got, ret, bottoms, back,
-    local_sem, halo_send, halo_recv, relay_send, relay_recv, fwd_send, fwd_recv, ret_send, ret_recv,
+    back,
+    frac, band, rows, s_0, uv_1, pq_1, s_1, uv_2, pq_2, s_2, uv_3, pq_3, s_3, turn, bound, share, surf,
+    relay, fwd, extra, s_4, got, ret, bottoms, bases,
+    local_sem, halo_send, halo_recv, relay_send, relay_recv, fwd_send, fwd_recv, ret_send, ret_recv, own_sem,
 ):
     lat, lev = lax.axis_index("lat"), lax.axis_index("lev")
     relayed = lat_size % RING == 0 and lat_size > RING
@@ -91,19 +107,6 @@
     lanes_in = lax.broadcasted_iota(jnp.int32, (8, 128), 1)
     small = sub < 4
 
-    def flip(x):
-        return pltpu.roll(x, 4, 0)
-
-    def transposed(xs):
-        for d in (4, 2, 1):
-            ys = list(xs)
-            for i in range(8):
-                if not i & d:
-                    ys[i] = jnp.where(sub & d == 0, xs[i], pltpu.roll(xs[i + d], d, 0))
-                    ys[i + d] = jnp.where(sub & d == 0, pltpu.roll(xs[i], 8 - d, 0), xs[i + d])
-            xs = ys
-        return xs
-
     for copy in own:
         copy.wait()
 
@@ -193,11 +196,11 @@
     for k in range(4 * PEERS):
         total = total + frac[k]
         share[k, :] = jnp.full((128,), frac[k], jnp.float32)
-        splat[k] = jnp.full((8, 128), frac[k], jnp.float32)
         bound[k, :] = jnp.full((128,), total, jnp.float32)
     share[...] = share[...] / total
     bound[...] = bound[...] / total
     bottoms[...] = jnp.zeros((8, 128), jnp.float32)
+    bases[...] = jnp.zeros((PEERS, 8, 128), jnp.float32)
     row_of = lax.broadcasted_iota(jnp.int32, (3 * ROWS, 8, 128), 0) + (lat - 1) * ROWS
     angle = -0.5 * math.pi + (row_of.astype(jnp.float32) + 0.5) * (math.pi / (lat_size * ROWS))
     sign = jnp.where(lax.broadcasted_iota(jnp.int32, (3 * ROWS, 8, 128), 1) < 4, ROTATION_RATE, -ROTATION_RATE)
@@ -343,13 +346,13 @@
                 got[4, lev, :, 0:PIECE] = extra[q, side]
 
     def ret_copy(q, step):
-        to = peer(step)
-        return remote(ret.at[q, to], back.at[q, lev], ret_send.at[q, step], ret_recv.at[q, step], (lat, to))
-
-    def last_copy(step):
-        to, lanes = peer(step), pl.ds(0, 512)
-        dst = back.at[4, lev, :, lanes]
-        return remote(ret.at[4, to, :, lanes], dst, ret_send.at[4, step], ret_recv.at[4, step], (lat, to))
+        to, lanes = peer(step), pl.ds(0, PAIR if q is None else 512)
+        n = 4 if q is None else q
+        dst = back.at[n, lev, :, lanes]
+        return remote(ret.at[n, to, :, lanes], dst, ret_send.at[n, step], ret_recv.at[n, step], (lat, to))
+
+    def own_copy(q):
+        return pltpu.make_async_copy(ret.at[q, lev], back.at[q, lev], own_sem.at[q])
 
     def running(values):
         out, carry = [], None
@@ -376,7 +379,7 @@
         first = side == 0
         row = jnp.where(q == 4, lev, jnp.where(first, 3 - q, 4 + q))
         t = jnp.where(q == 4, 8, lax.rem(lev - row + 2 * PEERS, PEERS))
-        at = side * PIECE
+        at, ret_at = side * PIECE, side * 256
 
         def split(n):
             xs = [got[q, p, :, pl.ds(pl.multiple_of(at + 128 * n, 128), 128)] for p in range(PEERS)]
@@ -430,7 +433,8 @@
         ]
         geo = [None] * 4
         ground = surf[:, pl.ds(pl.multiple_of(t * 128, 128), 128)]
-        carry = jnp.sum(jnp.where(sub == row, ground, 0.0), axis=0, keepdims=True)
+        ground_row = jnp.sum(jnp.where(sub == row, ground, 0.0), axis=0, keepdims=True)
+        carry = ground_row
         for i in (3, 2, 1, 0):
             x = rise[i]
             for d in (1, 2, 4):
@@ -438,24 +442,31 @@
             geo[i] = x + carry
             carry = geo[i][0:1]
         for n, (one, two) in enumerate(((remapped[0], remapped[1]), (remapped[2], remapped[3]))):
-            lanes = pl.ds(pl.multiple_of(at + 128 * n, 128), 128)
+            lanes = pl.ds(pl.multiple_of(ret_at + 128 * n, 128), 128)
             for i in range(4):
                 ret[q, 2 * i, :, lanes] = jnp.where(small, one[i], flip(two[i]))
                 ret[q, 2 * i + 1, :, lanes] = jnp.where(small, flip(one[i]), two[i])
-        mine = jnp.where(first, sub, 7 - sub) < 4
         floor = jnp.broadcast_to(bottom, (8, 128))
-        for i in range(4):
-            flipped = flip(geo[i])
-            for p, x in ((2 * i, jnp.where(first, geo[i], flipped)), (2 * i + 1, jnp.where(first, flipped, geo[i]))):
-                other = jnp.where(first, floor, ret[q, p, :, lane(2)])
-                ret[q, p, :, lane(2)] = jnp.where(mine, x, other)
-        bottoms[...] = jnp.where((sub == row) & (q < 4), floor, bottoms[...])
+        below = [x for i in range(4) for x in (geo[i][4:5], geo[i + 1][0:1] if i < 3 else ground_row)]
+
+        @pl.when(q < 4)
+        def _():
+            bottoms[...] = jnp.where(sub == row, floor, bottoms[...])
+            for p in range(PEERS):
+                bases[p] = jnp.where(sub == row, below[p], bases[p])
+
+        @pl.when(q == 4)
+        def _():
+            for p in range(PEERS):
+                ret[4, p, :, lane(2)] = jnp.where(small, floor, below[p])
+                ret[4, p, :, lane(3)] = bottoms[...]
+                ret[4, p, :, lane(4)] = bases[p]
 
     def process(q):
         lax.fori_loop(0, PEERS - 1, lambda k, z: (fwd_copy(q, k).wait_recv(), z)[1], 0)
         lax.fori_loop(0, 2, lambda side, z: (remap(q, side), z)[1], 0)
         lax.fori_loop(0, PEERS - 1, lambda k, z: (ret_copy(q, k).start(), z)[1], 0)
-        back[q, lev] = ret[q, lev]
+        own_copy(q).start()
 
     lax.fori_loop(5, 7, lambda m, z: (substep(1, 2 * m, 2 * m + 1), z)[1], 0)
 
@@ -489,49 +500,12 @@
     lax.fori_loop(2, 4, lambda q, z: (process(q), z)[1], 0)
     lax.fori_loop(0, PEERS - 1, lambda k, z: (extra_copy(0, 0, 0, k).wait_recv(), z)[1], 0)
     remap(4, 0)
-    for p in range(PEERS):
-        ret[4, p, :, lane(3)] = bottoms[...]
-    lax.fori_loop(0, PEERS - 1, lambda k, z: (last_copy(k).start(), z)[1], 0)
-    back[4, lev, :, 0:512] = ret[4, lev, :, 0:512]
-
-    for q in range(4):
+    lax.fori_loop(0, PEERS - 1, lambda k, z: (ret_copy(None, k).start(), z)[1], 0)
+    own_copy(4).start()
+    for q in (0, 1, 2, 3, None):
         lax.fori_loop(0, PEERS - 1, lambda k, z, q=q: (ret_copy(q, k).wait(), z)[1], 0)
-    lax.fori_loop(0, PEERS - 1, lambda k, z: (last_copy(k).wait(), z)[1], 0)
-
-    def put(lanes, uv, pq, geo, bottom):
-        for at, xs in ((0, uv), (64, pq)):
-            for i, x in enumerate(transposed(xs)):
-                out_ref[at + 8 * i : at + 8 * i + 8, lanes] = x
-        for i, x in enumerate(transposed(geo)[:4]):
-            out_geo_ref[8 * i : 8 * i + 8, lanes] = x
-            out_thick_ref[8 * i : 8 * i + 8, lanes] = bottom * (splat[4 * lev + i] / total)
-
-    def deliver(t, carry):
-        uv, pq, geo = [], [], []
-        bottom = jnp.zeros((8, 128), jnp.float32)
-        for r in range(ROWS):
-            owner, q, side = lax.rem(r + t, PEERS), max(3 - r, r - 4), r // 4
-            uv.append(back[q, owner, :, side * PIECE : side * PIECE + 128])
-            pq.append(back[q, owner, :, side * PIECE + 128 : side * PIECE + 256])
-            x = back[q, owner, :, lane(2)]
-            geo.append(flip(x) if side else x)
-            bottom = jnp.where(sub == r, back[4, owner, :, lane(3)], bottom)
-        put(pl.ds(pl.multiple_of(t * 128, 128), 128), uv, pq, geo, bottom)
-        return carry
-
-    lax.fori_loop(0, TILES - 1, deliver, 0)
-    geo = [back[4, r, :, lane(2)] for r in range(ROWS)]
-    bottom = jnp.zeros((8, 128), jnp.float32)
-    for r in range(ROWS):
-        bottom = jnp.where(sub == r, geo[r] if r >= 4 else flip(geo[r]), bottom)
-    put(
-        lane(8),
-        [back[4, r, :, lane(0)] for r in range(ROWS)],
-        [back[4, r, :, lane(1)] for r in range(ROWS)],
-        geo,
-        bottom,
-    )
-
+    for q in range(5):
+        own_copy(q).wait()
     for q in range(4):
         lax.fori_loop(0, PEERS - 1, lambda k, z, q=q: (fwd_copy(q, k).wait_send(), z)[1], 0)
     lax.fori_loop(0, PEERS - 1, lambda k, z: (extra_copy(0, 0, 0, k).wait_send(), z)[1], 0)
@@ -544,16 +518,72 @@
             pl.when(relays_north)(lambda h=h: forward_north(h).wait_send())
 
 
-def publish(remapped, thick, geo, out_ref, out_thick_ref, out_geo_ref, held, sem):
-    pairs = [(remapped.at[pl.ds(32 * n, 32)], out_ref.at[pl.ds(32 * n, 32)]) for n in range(4)]
-    pairs += [(thick, out_thick_ref), (geo, out_geo_ref)]
-    reads = [pltpu.make_async_copy(src, held.at[n], sem.at[0, n]) for n, (src, _) in enumerate(pairs)]
-    writes = [pltpu.make_async_copy(held.at[n], dst, sem.at[1, n]) for n, (_, dst) in enumerate(pairs)]
+def publish(back, frac_ref, out_ref, out_thick_ref, out_geo_ref, frac, held, out, thick, heights, read_sem, write_sem):
+    lev = lax.axis_index("lev")
+    fractions = pltpu.make_async_copy(frac_ref, frac, read_sem.at[5])
+    fractions.start()
+    reads = [pltpu.make_async_copy(back.at[n], held.at[n], read_sem.at[n]) for n in range(5)]
     for copy in reads:
         copy.start()
-    for read, write in zip(reads, writes):
-        read.wait()
-        write.start()
+    fractions.wait()
+
+    total, above = jnp.float32(0.0), [jnp.float32(0.0)] * 5
+    for k in range(4 * PEERS):
+        for i in range(5):
+            above[i] = jnp.where(k == 4 * lev + i, total, above[i])
+        total = total + frac[k]
+    above[4] = jnp.where(lev == PEERS - 1, total, above[4])
+    bounds = [jnp.full((8, 128), x, jnp.float32) / total for x in above]
+    shares = [jnp.full((8, 128), frac[4 * lev + i], jnp.float32) / total for i in range(4)]
+    sub = lax.broadcasted_iota(jnp.int32, (8, 128), 0)
+
+    def lane(t):
+        return slice(128 * t, 128 * t + 128)
+
+    def put(t, uv, pq, bottom, base):
+        lanes = lane(t)
+        uv, pq = transposed(uv), transposed(pq)
+        for i in range(8):
+            out[8 * i : 8 * i + 8, lanes] = uv[i]
+            out[64 + 8 * i : 72 + 8 * i, lanes] = pq[i]
+        pressure = [TOP_PRESSURE + bottom * x for x in bounds]
+        height = base
+        for i in (3, 2, 1, 0):
+            height = height + pq[i] * jnp.log(pressure[i + 1] / pressure[i])
+            heights[8 * i : 8 * i + 8, lanes] = height
+            thick[8 * i : 8 * i + 8, lanes] = bottom * shares[i]
+
+    def deliver(t):
+        uv, pq = [], []
+        bottom = base = jnp.zeros((8, 128), jnp.float32)
+        for r in range(ROWS):
+            owner, q, side = (r + t) % PEERS, max(3 - r, r - 4), r // 4
+            uv.append(held[q, owner, :, lane(2 * side)])
+            pq.append(held[q, owner, :, lane(2 * side + 1)])
+            bottom = jnp.where(sub == r, held[4, owner, :, lane(3)], bottom)
+            base = jnp.where(sub == r, held[4, owner, :, lane(4)], base)
+        put(t, uv, pq, bottom, base)
+
+    def deliver_last():
+        bottom = base = jnp.zeros((8, 128), jnp.float32)
+        for r in range(ROWS):
+            x = held[4, r, :, lane(2)]
+            bottom = jnp.where(sub == r, flip(x) if r >= 4 else x, bottom)
+            base = jnp.where(sub == r, x if r >= 4 else flip(x), base)
+        put(8, [held[4, r, :, lane(0)] for r in range(ROWS)], [held[4, r, :, lane(1)] for r in range(ROWS)], bottom, base)
+
+    for copy in reads:
+        copy.wait()
+    writes = []
+    for c in range(3):
+        for t in range(3 * c, min(3 * c + 3, TILES - 1)):
+            deliver(t)
+        if c == 2:
+            deliver_last()
+        lanes = pl.ds(384 * c, 384)
+        for n, (src, dst) in enumerate(((out, out_ref), (thick, out_thick_ref), (heights, out_geo_ref))):
+            writes.append(pltpu.make_async_copy(src.at[:, lanes], dst.at[:, lanes], write_sem.at[c, n]))
+            writes[-1].start()
     for copy in writes:
         copy.wait()
 
@@ -566,11 +596,11 @@
         jax.ShapeDtypeStruct((32, LON), f32),
         jax.ShapeDtypeStruct((32, LON), f32),
     )
-    results = pl.pallas_call(
+    returned = pl.pallas_call(
         functools.partial(kernel, lat_size),
-        out_shape=out_shape,
+        out_shape=jax.ShapeDtypeStruct((5, PEERS, 8, PAIR), f32),
         in_specs=[hbm] * 6,
-        out_specs=(pl.BlockSpec(memory_space=pltpu.VMEM),) * 3,
+        out_specs=hbm,
         scratch_shapes=[
             pltpu.SMEM((32,), f32),
             pltpu.VMEM((160, LON), f32),
@@ -579,7 +609,6 @@
             pltpu.VMEM((3 * ROWS, 8, 128), f32),
             pltpu.VMEM((32, 128), f32),
             pltpu.VMEM((32, 128), f32),
-            pltpu.VMEM((32, 8, 128), f32),
             pltpu.VMEM((ROWS, LON), f32),
             pltpu.VMEM((len(RELAYED), 8, ROW), f32),
             pltpu.VMEM((4, PEERS, 8, PAIR), f32),
@@ -588,7 +617,7 @@
             pltpu.VMEM((5, PEERS, 8, PAIR), f32),
             pltpu.VMEM((5, PEERS, 8, PAIR), f32),
             pltpu.VMEM((8, 128), f32),
-            pltpu.VMEM((5, PEERS, 8, PAIR), f32),
+            pltpu.VMEM((PEERS, 8, 128), f32),
             pltpu.SemaphoreType.DMA((6,)),
             pltpu.SemaphoreType.DMA((2, ROWS)),
             pltpu.SemaphoreType.DMA((2, ROWS)),
@@ -598,6 +627,7 @@
             pltpu.SemaphoreType.DMA((5, PEERS - 1)),
             pltpu.SemaphoreType.DMA((5, PEERS - 1)),
             pltpu.SemaphoreType.DMA((5, PEERS - 1)),
+            pltpu.SemaphoreType.DMA((5,)),
         ],
         compiler_params=pltpu.CompilerParams(
             collective_id=0, has_side_effects=True, vmem_limit_bytes=60 * 2**20
@@ -614,12 +644,20 @@
     remapped, new_thickness, geopotential = pl.pallas_call(
         publish,
         out_shape=out_shape,
-        in_specs=[hbm] * 3,
+        in_specs=[hbm] * 2,
         out_specs=(hbm,) * 3,
-        scratch_shapes=[pltpu.VMEM((6, 32, LON), f32), pltpu.SemaphoreType.DMA((2, 6))],
+        scratch_shapes=[
+            pltpu.SMEM((32,), f32),
+            pltpu.VMEM((5, PEERS, 8, PAIR), f32),
+            pltpu.VMEM((128, LON), f32),
+            pltpu.VMEM((32, LON), f32),
+            pltpu.VMEM((32, LON), f32),
+            pltpu.SemaphoreType.DMA((6,)),
+            pltpu.SemaphoreType.DMA((3, 3)),
+        ],
         compiler_params=pltpu.CompilerParams(vmem_limit_bytes=60 * 2**20),
         cost_estimate=pl.CostEstimate(flops=0, bytes_accessed=2 * 10**6, transcendentals=0),
-    )(*results)
+    )(returned, level_fractions)
     return (
         remapped.reshape(4, 4, ROWS, LON),
         new_thickness.reshape(4, ROWS, LON),

time: 44.9 us -> 43.9 us (0.978)
  Pallas kernels: 44.1 us -> 43.1 us
    pallas_call x2, Pallas kernels: 44.1 us -> 43.1 us  [the longest x1 40.8 us: shards(): pl.pallas_call(functools.partial(kernel, lat_size), out_shape=jax.ShapeDt...]
where the time goes in v5:
time: 43.9 us; the launch traced here: 43.8 us
  Pallas kernels  43.1 us (98%)
  between operations  0.64 us (1%)
    pallas_call x1, Pallas kernels, shards(): pl.pallas_call(functools.partial(kernel, lat_size), out_shape=jax.ShapeDt...  40.8 us
    pallas_call x1, Pallas kernels, shards(): pl.pallas_call(publish, out_shape=out_shape, in_specs=[hbm] * 2, out_spec...  2.32 us

profile of v5, /device:TPU:128, one launch (start us, length us, event | category | flops | bytes accessed | tf_op | source)
XLA Modules:
  0.0 43.8 jit_solution(8310263060972655715)
XLA Ops:
  0.6 40.8 %shard_map.85.back = f32[5,8,8,640]{3,2,1,0:T(8,128)} custom-call(f32[64,1152]{1,0:T(8,128)} %bitcast.8, f32[32,1152]{1,0:T(8,128)} %bitcast.9, f32[32,1152]{1,0:T(8,128)} %bitcast.10, f32[32,1152]{1,0:T(8,128)} %bitcast.11, f32[8,1152]{1,0:T(8,128)} %surf_ref.1, f32[32]{0:T(128)} %frac_ref.3), custom_call_target="tpu_custom_call" | custom-call | flops 100000000 | bytes 2000000 | tf_op jit(solution)/shard_map/pallas_call | solution.py:599
  41.4 2.3 %shard_map.86 = (f32[128,1152]{1,0:T(8,128)}, f32[32,1152]{1,0:T(8,128)}, f32[32,1152]{1,0:T(8,128)}) custom-call(f32[5,8,8,640]{3,2,1,0:T(8,128)} %shard_map.85.back, f32[32]{0:T(128)} %frac_ref.3), custom_call_target="tpu_custom_call" | custom-call | bytes 2000000 | tf_op jit(solution)/shard_map/pallas_call | solution.py:644

commit v6 on v5

--- a/solution.py
+++ b/solution.py
@@ -110,8 +110,8 @@
     for copy in own:
         copy.wait()
 
-    def unpack(t, carry):
-        at = pl.multiple_of(t * 128, 128)
+    def unpack(t):
+        at = t * 128
         for start, n in ((0, 0), (LON, 64)):
             xs = [band[n + 8 * i : n + 8 * i + 8, pl.ds(at, 128)] for i in range(8)]
             for r, x in enumerate(transposed(xs)):
@@ -119,9 +119,9 @@
         xs = [jnp.log(band[128 + 8 * i : 136 + 8 * i, pl.ds(at, 128)]) for i in range(4)]
         for r, x in enumerate(transposed(xs + xs)):
             s_0[ROWS + r, :, pl.ds(at, 128)] = x
-        return carry
-
-    lax.fori_loop(0, TILES, unpack, 0)
+
+    for t in range(TILES):
+        unpack(t)
 
     def fold(r, carry):
         j = ROWS + r

time: 43.9 us -> 43.9 us (level)
  no operation moved by 1% of the time
where the time goes in v6:
time: 43.9 us; the launch traced here: 43.8 us
  Pallas kernels  43.1 us (98%)
  between operations  0.64 us (1%)
    pallas_call x1, Pallas kernels, shards(): pl.pallas_call(functools.partial(kernel, lat_size), out_shape=jax.ShapeDt...  40.8 us
    pallas_call x1, Pallas kernels, shards(): pl.pallas_call(publish, out_shape=out_shape, in_specs=[hbm] * 2, out_spec...  2.32 us

profile of v6, /device:TPU:128, one launch (start us, length us, event | category | flops | bytes accessed | tf_op | source)
XLA Modules:
  0.0 43.8 jit_solution(8467892334432873027)
XLA Ops:
  0.6 40.8 %shard_map.85.back = f32[5,8,8,640]{3,2,1,0:T(8,128)} custom-call(f32[64,1152]{1,0:T(8,128)} %bitcast.8, f32[32,1152]{1,0:T(8,128)} %bitcast.9, f32[32,1152]{1,0:T(8,128)} %bitcast.10, f32[32,1152]{1,0:T(8,128)} %bitcast.11, f32[8,1152]{1,0:T(8,128)} %surf_ref.1, f32[32]{0:T(128)} %frac_ref.3), custom_call_target="tpu_custom_call" | custom-call | flops 100000000 | bytes 2000000 | tf_op jit(solution)/shard_map/pallas_call | solution.py:599
  41.4 2.3 %shard_map.86 = (f32[128,1152]{1,0:T(8,128)}, f32[32,1152]{1,0:T(8,128)}, f32[32,1152]{1,0:T(8,128)}) custom-call(f32[5,8,8,640]{3,2,1,0:T(8,128)} %shard_map.85.back, f32[32]{0:T(128)} %frac_ref.3), custom_call_target="tpu_custom_call" | custom-call | bytes 2000000 | tf_op jit(solution)/shard_map/pallas_call | solution.py:644
